TPU v7x, 128 devices: a whole 4x4x4 slice. The times are simulated.
128 devices in a mesh: row: 8 (over z, core), col: 16 (over y, x).
Axes of the slice: x: 4, y: 4, z: 4, core: 2. Of those that a mesh axis runs over, the one named last changes fastest.
Arguments:
- rest_pos: float32 [3, 262144], P(None, ('row', 'col')), may hold values from 0 to 4
- displacement: float32 [3, 262144], P(None, ('row', 'col')), may hold values from -1.2 to 1.2
- velocity: float32 [3, 262144], P(None, ('row', 'col')), may hold values from -3 to 3
- accel_prev: float32 [3, 262144], P(None, ('row', 'col')), may hold values from -6 to 6
- material: int32 [262144], P(('row', 'col')), may hold values from 0 to 1
- moduli: float32 [2], replicated, may hold values from 0.25 to 4
- pair_owner: int32 [16384], P(('row', 'col')), may hold values from 0 to 255, as said below
- pair_partner: int32 [16384], P(('row', 'col')), may hold values from 0 to 127, as said below
- pair_count: int32 [128], P(('row', 'col')), may hold values from 16 to 128, as said below
- bond_mask: int32 [16384, 128, 128], P(('row', 'col')), may hold values 0 or 1
- broken: int32 [16384, 128, 128], P(('row', 'col')), may hold values 0 or 1
Outputs:
- disp_out: float32 [3, 262144], P(None, ('row', 'col'))
- vel_out: float32 [3, 262144], P(None, ('row', 'col'))
Inputs may be any that keep to these rules, and one draw needn't show every extreme that they name: `pair_owner`: on each device the 128 slots name distinct tile pairs; over all devices no two tiles are joined by more than one slot, and no tile is joined with itself. `pair_partner`: drawn together with pair_owner. A device's live slots are its first pair_count slots; the lists and masks of the other slots are to be ignored. Some device has all 128 slots live.
All inputs are finite; a program needn't handle non-finite values. No bound on the sum of `bond_mask` or of `broken` on one device may be relied on, other than what follows from the above.
Results may differ from a plain program's by a relative error of at most 0.00011.
Values sent between devices are 32-bit elements; how exact they have to be, the bound alone decides.
No kernel may reach another device: no remote copies, remote signals or barrier semaphores. Data moves between devices by JAX's collectives and lax.ppermute only.
A program may use at most 64 MiB of HBM per device.

v0:
```python
import functools
import math

import jax
import jax.numpy as jnp
from jax import lax
from jax.experimental import pallas as pl
from jax.experimental.pallas import tpu as pltpu
from jax.sharding import PartitionSpec as P

TILE = 128
TILE_DEV = 16
PAIRS_DEV = 128
STEPS = 2
TIME_STEP = 0.5
CENTRE = 2.0
STRENGTH = 1.5 / math.sqrt(TILE * (1.0 + PAIRS_DEV / TILE_DEV))
UNROLL = 16
LEAD = 4
CORES = 2
LIMIT = 50 * 2**20
SMALL = 4 * 2**20
VMEM = pl.BlockSpec(memory_space=pltpu.VMEM)
ANY = pl.BlockSpec(memory_space=pltpu.HBM)
SMEM = pl.BlockSpec(memory_space=pltpu.SMEM)


def f32(*shape):
    return jax.ShapeDtypeStruct(shape, jnp.float32)


def rows_iota(n=8):
    return lax.broadcasted_iota(jnp.int32,(n,TILE),0)

def halves(c):
    c1=c.astype(jnp.bfloat16).astype(jnp.float32)
    return c1,(c-c1).astype(jnp.bfloat16).astype(jnp.float32)

def thirds(c):
    c1,c2=halves(c)
    return c1,c2,(c-c1)-c2

def row_of(s,k):
    return jnp.broadcast_to(s[k:k+1],(8,TILE))

def features(s,owner,alive=None):
    r=rows_iota()
    f=row_of(s,7); m=row_of(s,3)
    if alive is not None:
        m=m*alive
    c1,c2=halves(jnp.where(r==3,f*row_of(s,4),s))
    c=c1+c2
    sq=c*c
    w=jnp.where(r==3,sq,sq+pltpu.roll(sq,7,0)+pltpu.roll(sq,6,0)+0.5)
    z1,z2=halves(m*jnp.where(r==3,1.0,s))
    z=jnp.where(r<4,z1,pltpu.roll(z2,4,0))
    z=jnp.concatenate([z,jnp.zeros_like(z)],0).astype(jnp.bfloat16)
    if owner:
        ones=jnp.where(r==5,f,1.0)
        n=[jnp.where((r==0)|(r==3)|(r==4),t,ones) for t in thirds(w)]
        x=[c1,c1,c2,c2]+n+[jnp.zeros_like(ones)]
    else:
        ones=jnp.where(r==3,f,1.0)
        n=[jnp.where((r==2)|(r==5)|(r==6),t,ones) for t in thirds(pltpu.roll(w,2,0))]
        x=[c1,c2,c1,c2]+n+[jnp.zeros_like(ones)]
    return jnp.concatenate(x,0).astype(jnp.bfloat16),z,m

def patterns():
    row=lax.broadcasted_iota(jnp.int32,(64,TILE),0)
    coord=row<32; spare=row>=56
    row=row%8
    def pick(lo,hi,n1,n2,scale):
        c=jnp.where((row>=lo)&(row<hi),-2.0*scale,0.0)
        n=jnp.where((row==n1)|(row==n2),scale,0.0)
        return jnp.where(spare,0.0,jnp.where(coord,c,n))
    now=pick(0,3,0,2,1.0); rest=pick(4,7,4,6,1.0)
    return now,rest,rest+pick(3,4,3,5,8.0)

def post(acc,s,m):
    t=acc[:8,:TILE]+acc[:8,TILE:]
    t=t+pltpu.roll(t,4,0)
    return (STRENGTH*m)*(t-s*row_of(t,3))

def lengths(left, base, pat_ref, groups=3):
    right = jnp.concatenate([base * pat_ref[k] for k in range(groups)], 1)
    return lax.dot_general(left, right, (((0,), (0,)), ((), ())), preferred_element_type=jnp.float32)


def inverse_lengths(d):
    return lax.rsqrt(jnp.maximum(d[:, :TILE], 1.0)), lax.rsqrt(d[:, TILE:2 * TILE])


def stiffness(d, inv_rest):
    return d[:, 2 * TILE:] * (inv_rest * inv_rest)


def weights(inv_now, inv_rest, stiff):
    w = (inv_rest - inv_now) * stiff
    high = w.astype(jnp.bfloat16)
    return high, (w - high.astype(jnp.float32)).astype(jnp.bfloat16)


def sum_owner(z,w):
    return lax.dot_general(z,jnp.concatenate(w,0),(((1,),(1,)),((),())),preferred_element_type=jnp.float32)

def sum_partner(z,w):
    return jnp.dot(z,jnp.concatenate(w,1),preferred_element_type=jnp.float32)

def pair_kernel(n_row, fresh, ids_ref, *refs):
    if fresh:
        bond_ref, broken_ref, row_ref = refs[:3]
        col_refs = refs[3:2 + n_row]
        rowf_ref, mine_ref, sibling_ref, all_rows_ref, all_cols_ref, all_stiff_ref = refs[2 + n_row:8 + n_row]
        refs = refs[8 + n_row:]
    else:
        all_rows_ref, all_cols_ref, all_stiff_ref, row_ref = refs[:4]
        col_refs = refs[4:3 + n_row]
        rowf_ref, mine_ref, sibling_ref = refs[3 + n_row:6 + n_row]
        refs = refs[6 + n_row:]
    list_ref, pat_ref, rows_ref, cols_ref, colf_ref, stiff_ref, d_ref, z_ref, sems, list_sem, state_sems = refs[:11]
    if fresh:
        bonds_ref, cracks_ref, out_sems = refs[11:]
    n_col, n_z = row_ref.shape[0], n_row // CORES
    full = 8 * TILE_DEV
    part = 3 * TILE_DEV
    at_row = lax.axis_index("row")
    z, core = at_row // CORES, at_row % CORES
    fetch = pltpu.make_async_copy(ids_ref, list_ref, list_sem)
    fetch.start()
    if fresh:
        states = (
            pltpu.make_async_copy(rows_ref, all_rows_ref, state_sems.at[0]),
            pltpu.make_async_copy(cols_ref, all_cols_ref, state_sems.at[1]),
        )
    else:
        states = (
            pltpu.make_async_copy(all_rows_ref, rows_ref, state_sems.at[0]),
            pltpu.make_async_copy(all_cols_ref, cols_ref, state_sems.at[1]),
        )
        for copy in states:
            copy.start()
    for k, p in enumerate(patterns()):
        pat_ref[k] = p.astype(jnp.bfloat16)
    fetch.wait()
    live = list_ref[2, 0].astype(jnp.int32)
    chunks = (live + UNROLL - 1) // UNROLL

    def copies(i):
        part = pl.ds(i * UNROLL, UNROLL)
        if not fresh:
            return (pltpu.make_async_copy(all_stiff_ref.at[part], stiff_ref.at[part], sems.at[0, i]),)
        return (
            pltpu.make_async_copy(bond_ref.at[part], bonds_ref.at[part], sems.at[0, i]),
            pltpu.make_async_copy(broken_ref.at[part], cracks_ref.at[part], sems.at[1, i]),
        )

    def store(i):
        part = pl.ds(i * UNROLL, UNROLL)
        return pltpu.make_async_copy(stiff_ref.at[part], all_stiff_ref.at[part], out_sems.at[i])

    def begin(i, carry):
        for copy in copies(i):
            copy.start()
        return carry

    lax.fori_loop(0, chunks, begin, 0)
    rowf_ref[...] = jnp.zeros_like(rowf_ref)
    colf_ref[...] = jnp.zeros_like(colf_ref)
    if not fresh:
        for copy in states:
            copy.wait()
    roots = (list_ref[3, 0], list_ref[4, 0])

    def place(ref, at, block):
        if not fresh:
            ref[pl.ds(at, part)] = block.reshape(part, TILE)
            return
        ref[pl.ds(at, part)] = block[:3].reshape(part, TILE)
        ref[pl.ds(at + part, TILE_DEV)] = jnp.where(block[6] == 1.0, roots[1], roots[0])
        ref[pl.ds(at + part + TILE_DEV, part + TILE_DEV)] = block[3:].reshape(part + TILE_DEV, TILE)

    for c in range(n_col):
        place(rows_ref, c * full, row_ref[c])
    for d in range(n_z):
        src = (z + n_z - d) % n_z
        for j in range(CORES):
            k = d * CORES + j
            block = row_ref[lax.axis_index("col")] if k == 0 else col_refs[k - 1][...]
            r = src * CORES + (core if j == 0 else 1 - core)
            place(cols_ref, pl.multiple_of(r * full, full), block)
    if fresh:
        for copy in states:
            copy.start()

    def load(ref, t):
        return ref[pl.ds((t // TILE_DEV) * full + t % TILE_DEV, 8, stride=TILE_DEV), :]

    def add(ref, t, val):
        where = pl.ds((t // TILE_DEV) * part + t % TILE_DEV, 3, stride=TILE_DEV)
        ref[where, :] = ref[where, :] + val[:3]

    own = []
    for j in range(TILE_DEV):
        t = lax.axis_index("col") * TILE_DEV + j
        state = load(rows_ref, t)
        own.append((t, state, features(state, True), features(state, False)))
    ahead = {}
    for j in range(TILE_DEV + LEAD):
        if j < TILE_DEV:
            ahead[j] = lengths(own[j][2][0], own[j][3][0], pat_ref)
        if j >= LEAD:
            t, state, mine, other = own[j - LEAD]
            d = ahead.pop(j - LEAD)
            inv_now, inv_rest = inverse_lengths(d)
            on_owner = sum_owner(other[1], weights(inv_now, inv_rest, stiffness(d, inv_rest)))
            add(rowf_ref, t, post(on_owner, state, mine[2]))

    def pair(slot):
        return list_ref[0, slot].astype(jnp.int32), list_ref[1, slot].astype(jnp.int32)

    def tiles(slot):
        o, p = pair(slot)
        return load(rows_ref, o), load(cols_ref, p)

    groups = 3 if fresh else 2

    def begin_pair(slot):
        alive = jnp.where(slot < live, 1.0, 0.0)
        so, sp = tiles(jnp.minimum(slot, PAIRS_DEV - 1))
        fo, fp = features(so, True, alive), features(sp, False, alive)
        return lengths(fo[0], fp[0], pat_ref, groups), fo[1], fp[1]

    def keep(j, begun):
        d_ref[j] = begun[0]
        z_ref[j, 0] = begun[1]
        z_ref[j, 1] = begun[2]

    for j in range(LEAD):
        keep(j, begin_pair(j))

    def body(i, carry):
        for copy in copies(i):
            copy.wait()
        first = i * UNROLL
        begun = {j: (d_ref[j], z_ref[j, 0], z_ref[j, 1]) for j in range(LEAD)}
        sums = []
        for j in range(UNROLL):
            if j + LEAD < UNROLL:
                begun[j + LEAD] = begin_pair(first + j + LEAD)
            d, zo, zp = begun.pop(j)
            inv_now, inv_rest = inverse_lengths(d)
            if fresh:
                stiff = jnp.where(bonds_ref[first + j] > cracks_ref[first + j], stiffness(d, inv_rest), 0.0)
                stiff_ref[first + j] = stiff
            else:
                stiff = stiff_ref[first + j]
            w = weights(inv_now, inv_rest, stiff)
            sums.append((sum_owner(zp, w), sum_partner(zo, w)))
            if j + LEAD >= UNROLL:
                keep(j + LEAD - UNROLL, begin_pair(first + j + LEAD))
        for j, (on_owner, on_partner) in enumerate(sums):
            so, sp = tiles(first + j)
            alive = jnp.where(first + j < live, 1.0, 0.0)
            o, p = pair(first + j)
            add(rowf_ref, o, post(on_owner, so, row_of(so, 3) * alive))
            add(colf_ref, p, post(on_partner, sp, row_of(sp, 3) * alive))
        if fresh:
            store(i).start()
        return carry

    lax.fori_loop(0, chunks, body, 0)
    for i in range(n_z):
        for ref, c in ((mine_ref, core), (sibling_ref, 1 - core)):
            start = pl.multiple_of((i * CORES + c) * part, part)
            ref[i] = colf_ref[pl.ds(start, part)].reshape(3, TILE_DEV, TILE)
    if fresh:
        def finish(i, carry):
            store(i).wait()
            return carry

        lax.fori_loop(0, chunks, finish, 0)
        for copy in states:
            copy.wait()


def pair_forces(ids, row, cols, masks=(), states=()):
    n_col, n_row = row.shape[0], len(cols) + 1
    n_z = n_row // CORES
    fresh = not states
    chunks = PAIRS_DEV // UNROLL
    shares = f32(n_z, 3, TILE_DEV, TILE)
    out = (f32(n_col * 3 * TILE_DEV, TILE), shares, shares)
    held = (f32(n_col * 8 * TILE_DEV, TILE), f32(n_row * 8 * TILE_DEV, TILE), f32(PAIRS_DEV, TILE, TILE))
    inputs = masks if fresh else states
    return pl.pallas_call(
        functools.partial(pair_kernel, n_row, fresh),
        out_shape=out + held if fresh else out,
        in_specs=[ANY] * (1 + len(inputs)) + [VMEM] * n_row,
        out_specs=(VMEM,) * 3 + ((ANY,) * 3 if fresh else ()),
        scratch_shapes=[
            pltpu.SMEM(ids.shape, ids.dtype),
            pltpu.VMEM((3, 64, TILE), jnp.bfloat16),
            pltpu.VMEM(held[0].shape, jnp.float32),
            pltpu.VMEM(held[1].shape, jnp.float32),
            pltpu.VMEM((n_row * 3 * TILE_DEV, TILE), jnp.float32),
            pltpu.VMEM(held[2].shape, jnp.float32),
            pltpu.VMEM((LEAD, TILE, (3 if fresh else 2) * TILE), jnp.float32),
            pltpu.VMEM((LEAD, 2, 16, TILE), jnp.bfloat16),
            pltpu.SemaphoreType.DMA((2, chunks)),
            pltpu.SemaphoreType.DMA,
            pltpu.SemaphoreType.DMA((2,)),
        ] + ([pltpu.VMEM(mask.shape, mask.dtype) for mask in masks] + [pltpu.SemaphoreType.DMA((chunks,))] if fresh else []),
        compiler_params=pltpu.CompilerParams(vmem_limit_bytes=LIMIT),
        name="pair_forces" if fresh else "pair_forces_again",
    )(ids, *inputs, row, *cols)


def start_kernel(
    moduli_ref, count_ref, owner_ref, partner_ref, material_ref, rest_ref, disp_ref, vel_ref, acc_ref,
    spread_ref, state_ref, u_ref, v_ref, ids_ref
):
    ids_ref[0:1] = owner_ref[...].astype(jnp.float32)
    ids_ref[1:2] = partner_ref[...].astype(jnp.float32)
    ids_ref[2:3] = jnp.full((1, TILE), count_ref[0], jnp.int32).astype(jnp.float32)
    for k in range(2):
        ids_ref[3 + k:4 + k] = jnp.sqrt(jnp.full((1, TILE), moduli_ref[k]))
    for c in range(3):
        for t in range(TILE_DEV):
            lanes = pl.ds(t * TILE, TILE)
            v = vel_ref[c:c + 1, lanes] + 0.5 * TIME_STEP * acc_ref[c:c + 1, lanes]
            u = disp_ref[c:c + 1, lanes] + TIME_STEP * v
            x = rest_ref[c:c + 1, lanes] - CENTRE
            v_ref[c, t:t + 1, :] = v
            u_ref[c, t:t + 1, :] = u
            state_ref[c, t:t + 1, :] = x + u
            state_ref[3 + c, t:t + 1, :] = x
    state_ref[6] = material_ref[...].astype(jnp.float32)
    for i in range(spread_ref.shape[0]):
        spread_ref[i] = state_ref[...]


def start(n_col, moduli, count, owner, partner, material, rest, disp, vel, acc):
    block = (3, TILE_DEV, TILE)
    return pl.pallas_call(
        start_kernel,
        out_shape=(f32(n_col, 7, TILE_DEV, TILE), f32(7, TILE_DEV, TILE), f32(*block), f32(*block),
                   f32(5, TILE)),
        in_specs=[SMEM] * 2 + [VMEM] * 7,
        out_specs=(VMEM,) * 5,
        name="first_half_step",
    )(moduli, count, owner, partner, material, rest, disp, vel, acc)


def share_kernel(mine_ref, other_ref, *out_refs):
    n_z = len(out_refs)
    z = lax.axis_index("row") // CORES
    for d, out_ref in enumerate(out_refs):
        at = (z + d) % n_z
        out_ref[...] = mine_ref[at] + other_ref[at]


def shares(mine, other):
    n_z = mine.shape[0]
    return pl.pallas_call(
        share_kernel,
        out_shape=(f32(*mine.shape[1:]),) * n_z,
        in_specs=[VMEM] * 2,
        out_specs=(VMEM,) * n_z,
        compiler_params=pltpu.CompilerParams(vmem_limit_bytes=SMALL),
        name="column_shares",
    )(mine, other)


def total(row_ref, col_refs):
    force = row_ref[0]
    for i in range(1, row_ref.shape[0]):
        force = force + row_ref[i]
    for ref in col_refs:
        force = force + ref[...]
    return force


def step_kernel(n_z, row_ref, *refs):
    col_refs = refs[:n_z]
    state_ref, u_ref, v_ref, spread_ref, now_ref, new_u_ref, new_v_ref = refs[n_z:]
    force = total(row_ref, col_refs)
    v = v_ref[...] + TIME_STEP * force
    u = u_ref[...] + TIME_STEP * v
    now = state_ref[3:6] + u
    new_u_ref[...] = u
    new_v_ref[...] = v
    now_ref[...] = now
    for i in range(spread_ref.shape[0]):
        spread_ref[i] = now


def next_step(row, cols, state, u, v):
    return pl.pallas_call(
        functools.partial(step_kernel, len(cols)),
        out_shape=(f32(*row.shape),) + (f32(*u.shape),) * 3,
        in_specs=[VMEM] * (4 + len(cols)),
        out_specs=(VMEM,) * 4,
        compiler_params=pltpu.CompilerParams(vmem_limit_bytes=SMALL),
        name="next_step",
    )(row, *cols, state, u, v)


def last_kernel(n_z, row_ref, *refs):
    col_refs = refs[:n_z]
    u_ref, v_ref, disp_ref, vel_ref = refs[n_z:]
    v = v_ref[...] + 0.5 * TIME_STEP * total(row_ref, col_refs)
    for c in range(3):
        for t in range(TILE_DEV):
            lanes = pl.ds(t * TILE, TILE)
            disp_ref[c:c + 1, lanes] = u_ref[c, t:t + 1, :]
            vel_ref[c:c + 1, lanes] = v[c, t:t + 1, :]


def last_step(row, cols, u, v):
    points = f32(3, TILE_DEV * TILE)
    return pl.pallas_call(
        functools.partial(last_kernel, len(cols)),
        out_shape=(points, points),
        in_specs=[VMEM] * (3 + len(cols)),
        out_specs=(VMEM,) * 2,
        compiler_params=pltpu.CompilerParams(vmem_limit_bytes=SMALL),
        name="last_half_step",
    )(row, *cols, u, v)


def to_sibling(x, n_row):
    return lax.ppermute(x, "row", [(i, i ^ 1) for i in range(n_row)])


def along_z(x, d, n_row):
    n_z = n_row // CORES
    return lax.ppermute(x, "row", [(i, (i // CORES + d) % n_z * CORES + i % CORES) for i in range(n_row)])


def swap(x):
    return lax.all_to_all(x, "col", 0, 0, tiled=True)


def column_gather(block, n_row):
    blocks = [block] + [along_z(block, d, n_row) for d in range(1, n_row // CORES)]
    return [x for mine in blocks for x in (mine, to_sibling(mine, n_row))][1:]


def column_sum(mine, sibling, n_row):
    parts = shares(mine, to_sibling(sibling, n_row))
    return [parts[0]] + [along_z(parts[d], d, n_row) for d in range(1, n_row // CORES)]


def per_device(
    rest_pos, displacement, velocity, accel_prev, material, moduli, pair_owner, pair_partner, pair_count, bond_mask, broken
):
    n_row, n_col = lax.axis_size("row"), lax.axis_size("col")
    spread, state, u, v, ids = start(
        n_col, moduli, pair_count, pair_owner.reshape(1, -1), pair_partner.reshape(1, -1),
        material.reshape(TILE_DEV, TILE), rest_pos, displacement, velocity, accel_prev
    )
    row, cols, states = swap(spread), column_gather(state, n_row), ()
    for step in range(STEPS):
        rowf, mine, sibling, *held = pair_forces(ids, row, cols, (bond_mask, broken), states)
        row_part = swap(rowf.reshape(n_col, 3, TILE_DEV, TILE))
        col_part = column_sum(mine, sibling, n_row)
        if step < STEPS - 1:
            spread, block, u, v = next_step(row_part, col_part, state, u, v)
            row, cols, states = swap(spread), column_gather(block, n_row), tuple(held)
    return last_step(row_part, col_part, u, v)


def solution(mesh):
    points, flat, masks = P(None, ("row", "col")), P(("row", "col")), P(("row", "col"), None, None)
    return jax.shard_map(
        per_device,
        mesh=mesh,
        in_specs=(points,) * 4 + (flat, P()) + (flat,) * 3 + (masks,) * 2,
        out_specs=(points, points),
        check_vma=False,
    )
```

profile of v0, /device:TPU:0, one launch (start us, length us, event | category | flops | bytes accessed | tf_op | source)
XLA Modules:
  0.0 90.7 jit_solution(10749179083657959146)
XLA Ops:
  1.3 2.0 %first_half_step.1 = (f32[16,7,16,128]{3,2,1,0:T(8,128)}, f32[7,16,128]{2,1,0:T(8,128)}, f32[3,16,128]{2,1,0:T(8,128)}, f32[3,16,128]{2,1,0:T(8,128)}, f32[5,128]{1,0:T(8,128)}) custom-call(f32[2]{0:T(128)} %moduli_ref.1, s32[1]{0:T(128)S(6)} %copy.13.count_ref, s32[1,128]{1,0:T(1,128)} %bitcast.6, s32[1,128]{1,0:T(1,128)} %bitcast.7, s32[16,128]{1,0:T(8,128)} %bitcast.5, ...), custom_call_target="tpu_custom_call" | custom-call | tf_op jit(solution)/shard_map/first_half_step/pallas_call | solution.py:344
  3.2 7.1 %all-to-all-start = ((f32[16,7,16,128]{3,2,1,0:T(8,128)}), f32[16,7,16,128]{3,2,1,0:T(8,128)S(1)}, u32[]{:S(2)}, u32[]{:S(2)}) async-start(f32[16,7,16,128]{3,2,1,0:T(8,128)} %get-tuple-element.29), calls=%async_computation | async-start | bytes 1835008 | tf_op jit(solution)/shard_map/all_to_all | solution.py:441
  10.4 4.1 %collective-permute-start.5 = (f32[7,16,128]{2,1,0:T(8,128)}, f32[7,16,128]{2,1,0:T(8,128)S(1)}, u32[]{:S(2)}, u32[]{:S(2)}) collective-permute-start(f32[7,16,128]{2,1,0:T(8,128)} %get-tuple-element.30.refs_4_), channel_id=1, source_target_pairs={{0,96},{16,112},{32,0},{48,16},{64,32},{80,48},{96,64},{112,80},{1... | collective-permute-start | bytes 172040 | tf_op jit(solution)/shard_map/ppermute | solution.py:437
  14.5 1.3 %collective-permute-start.1 = (f32[7,16,128]{2,1,0:T(8,128)}, f32[7,16,128]{2,1,0:T(8,128)S(1)}, u32[]{:S(2)}, u32[]{:S(2)}) collective-permute-start(f32[7,16,128]{2,1,0:T(8,128)} %get-tuple-element.30.refs_4_), channel_id=1, source_target_pairs={{0,32},{16,48},{32,64},{48,80},{64,96},{80,112},{96,0},{112,16},{1... | collective-permute-start | bytes 172040 | tf_op jit(solution)/shard_map/ppermute | solution.py:437
  15.7 0.9 collective-permute-done.5.refs_8_
  16.6 0.0 collective-permute-start.6
  16.6 3.8 %collective-permute-done.3.refs_6_ = f32[7,16,128]{2,1,0:T(8,128)S(1)} collective-permute-done((f32[7,16,128]{2,1,0:T(8,128)}, f32[7,16,128]{2,1,0:T(8,128)S(1)}, u32[]{:S(2)}, u32[]{:S(2)}) %collective-permute-start.3) | collective-permute-done | bytes 57376 | tf_op jit(solution)/shard_map/ppermute | solution.py:437
  20.4 0.3 collective-permute-done.1.refs_4_
  20.7 0.2 collective-permute-start.2
  20.9 0.7 collective-permute-done.4.refs_7_
  21.7 0.3 collective-permute-done.2.refs_5_
  21.9 4.5 %all-to-all-done.refs_2_ = f32[16,7,16,128]{3,2,1,0:T(8,128)S(1)} async-done(((f32[16,7,16,128]{3,2,1,0:T(8,128)}), f32[16,7,16,128]{3,2,1,0:T(8,128)S(1)}, u32[]{:S(2)}, u32[]{:S(2)}) %all-to-all-start) | async-done | bytes 917536 | tf_op jit(solution)/shard_map/all_to_all | solution.py:441
  26.4 0.7 copy-done.3
  27.1 6.0 %pair_forces.1 = (f32[768,128]{1,0:T(8,128)}, f32[4,3,16,128]{3,2,1,0:T(8,128)S(1)}, f32[4,3,16,128]{3,2,1,0:T(8,128)S(1)}, f32[2048,128]{1,0:T(8,128)S(1)}, f32...) custom-call(f32[5,128]{1,0:T(8,128)S(1)} %copy-done.3, s32[128,128,128]{2,1,0:T(8,128)} %refs_0_.1, ...), custom_call_target="tpu_custom_call" | custom-call | tf_op jit(solution)/shard_map/pair_forces/pallas_call | solution.py:295
  33.1 4.7 %all-to-all-start.1 = ((f32[16,3,16,128]{3,2,1,0:T(8,128)}), f32[16,3,16,128]{3,2,1,0:T(8,128)S(1)}, u32[]{:S(2)}, u32[]{:S(2)}) async-start(f32[16,3,16,128]{3,2,1,0:T(8,128)} %bitcast.3), calls=%async_computation.1 | async-start | bytes 786432 | tf_op jit(solution)/shard_map/all_to_all | solution.py:441
  37.8 0.1 collective-permute-start.7
  37.9 1.3 %collective-permute-done.7.other_ref = f32[4,3,16,128]{3,2,1,0:T(8,128)S(1)} collective-permute-done((f32[4,3,16,128]{3,2,1,0:T(8,128)S(1)}, f32[4,3,16,128]{3,2,1,0:T(8,128)S(1)}, u32[]{:S(2)}, u32[]{:S(2)}) %collective-permute-start.7) | collective-permute-done | bytes 98336 | tf_op jit(solution)/shard_map/ppermute | solution.py:432
  39.2 2.9 %collective-permute-start.8 = (f32[3,16,128]{2,1,0:T(8,128)S(1)}, f32[3,16,128]{2,1,0:T(8,128)S(1)}, u32[]{:S(2)}, u32[]{:S(2)}) collective-permute-start(f32[3,16,128]{2,1,0:T(8,128)S(1)} %get-tuple-element.38), channel_id=1, source_target_pairs={{0,32},{16,48},{32,64},{48,80},{64,96},{80,112},{96,0},{112,16},{1... | collective-permute-start | bytes 73736 | tf_op jit(solution)/shard_map/ppermute | solution.py:437
  42.1 3.6 %collective-permute-start.9 = (f32[3,16,128]{2,1,0:T(8,128)S(1)}, f32[3,16,128]{2,1,0:T(8,128)S(1)}, u32[]{:S(2)}, u32[]{:S(2)}) collective-permute-start(f32[3,16,128]{2,1,0:T(8,128)S(1)} %get-tuple-element.39), channel_id=1, source_target_pairs={{0,64},{16,80},{32,96},{48,112},{64,0},{80,16},{96,32},{112,48},{1... | collective-permute-start | bytes 73736 | tf_op jit(solution)/shard_map/ppermute | solution.py:437
  45.6 0.9 collective-permute-start.10
  46.5 0.0 collective-permute-done.8.refs_1_
  46.5 1.2 %collective-permute-done.9.refs_2_ = f32[3,16,128]{2,1,0:T(8,128)S(1)} collective-permute-done((f32[3,16,128]{2,1,0:T(8,128)S(1)}, f32[3,16,128]{2,1,0:T(8,128)S(1)}, u32[]{:S(2)}, u32[]{:S(2)}) %collective-permute-start.9) | collective-permute-done | bytes 24608 | tf_op jit(solution)/shard_map/ppermute | solution.py:437
  47.7 1.8 %collective-permute-done.10.refs_3_ = f32[3,16,128]{2,1,0:T(8,128)S(1)} collective-permute-done((f32[3,16,128]{2,1,0:T(8,128)S(1)}, f32[3,16,128]{2,1,0:T(8,128)S(1)}, u32[]{:S(2)}, u32[]{:S(2)}) %collective-permute-start.10) | collective-permute-done | bytes 24608 | tf_op jit(solution)/shard_map/ppermute | solution.py:437
  49.5 0.0 all-to-all-done.1.row_ref
  49.5 0.9 next_step.1
  50.3 7.1 %all-to-all-start.2 = ((f32[16,3,16,128]{3,2,1,0:T(8,128)}), f32[16,3,16,128]{3,2,1,0:T(8,128)S(1)}, u32[]{:S(2)}, u32[]{:S(2)}) async-start(f32[16,3,16,128]{3,2,1,0:T(8,128)} %get-tuple-element.43), calls=%async_computation.2 | async-start | bytes 786432 | tf_op jit(solution)/shard_map/all_to_all | solution.py:441
  57.4 1.9 %collective-permute-start.16 = (f32[3,16,128]{2,1,0:T(8,128)S(1)}, f32[3,16,128]{2,1,0:T(8,128)S(1)}, u32[]{:S(2)}, u32[]{:S(2)}) collective-permute-start(f32[3,16,128]{2,1,0:T(8,128)S(1)} %get-tuple-element.44), channel_id=1, source_target_pairs={{0,96},{16,112},{32,0},{48,16},{64,32},{80,48},{96,64},{112,80},{1... | collective-permute-start | bytes 73736 | tf_op jit(solution)/shard_map/ppermute | solution.py:437
  59.4 0.0 collective-permute-start.14
  59.4 1.1 %collective-permute-start.12 = (f32[3,16,128]{2,1,0:T(8,128)S(1)}, f32[3,16,128]{2,1,0:T(8,128)S(1)}, u32[]{:S(2)}, u32[]{:S(2)}) collective-permute-start(f32[3,16,128]{2,1,0:T(8,128)S(1)} %get-tuple-element.44), channel_id=1, source_target_pairs={{0,32},{16,48},{32,64},{48,80},{64,96},{80,112},{96,0},{112,16},{1... | collective-permute-start | bytes 73736 | tf_op jit(solution)/shard_map/ppermute | solution.py:437
  60.4 0.0 collective-permute-start.11
  60.4 0.9 collective-permute-done.16.refs_9_
  61.3 3.4 %collective-permute-done.14.refs_7_ = f32[3,16,128]{2,1,0:T(8,128)S(1)} collective-permute-done((f32[3,16,128]{2,1,0:T(8,128)S(1)}, f32[3,16,128]{2,1,0:T(8,128)S(1)}, u32[]{:S(2)}, u32[]{:S(2)}) %collective-permute-start.14) | collective-permute-done | bytes 24608 | tf_op jit(solution)/shard_map/ppermute | solution.py:437
  64.7 0.5 collective-permute-start.13
  65.2 0.7 collective-permute-done.15.refs_8_
  65.9 0.2 collective-permute-done.13.refs_6_
  66.1 0.8 all-to-all-done.2.refs_3_
  66.8 4.6 %pair_forces_again.1 = (f32[768,128]{1,0:T(8,128)}, f32[4,3,16,128]{3,2,1,0:T(8,128)S(1)}, f32[4,3,16,128]{3,2,1,0:T(8,128)S(1)}) custom-call(f32[5,128]{1,0:T(8,128)S(1)} %copy-done.4, f32[2048,128]{1,0:T(8,128)S(1)} %get-tuple-element.31.refs_0_, f32[1024,128]{1,0:T(8,128)S(1)} %get-tuple-element.32.refs_1_, f32[128,128,128]{2,1,0:T(8,128)} %get-tuple-element.33.refs_2_, ...), custom_call_target="tpu_custom_call" | custom-call | tf_op jit(solution)/shard_map/pair_forces_again/pallas_call | solution.py:295
  71.5 8.3 %all-to-all-start.3 = ((f32[16,3,16,128]{3,2,1,0:T(8,128)}), f32[16,3,16,128]{3,2,1,0:T(8,128)S(1)}, u32[]{:S(2)}, u32[]{:S(2)}) async-start(f32[16,3,16,128]{3,2,1,0:T(8,128)} %bitcast.4), calls=%async_computation.3 | async-start | bytes 786432 | tf_op jit(solution)/shard_map/all_to_all | solution.py:441
  79.7 0.1 collective-permute-start.18
  79.8 1.3 %collective-permute-done.18.other_ref = f32[4,3,16,128]{3,2,1,0:T(8,128)S(1)} collective-permute-done((f32[4,3,16,128]{3,2,1,0:T(8,128)S(1)}, f32[4,3,16,128]{3,2,1,0:T(8,128)S(1)}, u32[]{:S(2)}, u32[]{:S(2)}) %collective-permute-start.18) | collective-permute-done | bytes 98336 | tf_op jit(solution)/shard_map/ppermute | solution.py:432
  81.1 0.1 collective-permute-start.19
  81.2 1.9 %collective-permute-start.20 = (f32[3,16,128]{2,1,0:T(8,128)S(1)}, f32[3,16,128]{2,1,0:T(8,128)S(1)}, u32[]{:S(2)}, u32[]{:S(2)}) collective-permute-start(f32[3,16,128]{2,1,0:T(8,128)S(1)} %get-tuple-element.50), channel_id=1, source_target_pairs={{0,64},{16,80},{32,96},{48,112},{64,0},{80,16},{96,32},{112,48},{1... | collective-permute-start | bytes 73736 | tf_op jit(solution)/shard_map/ppermute | solution.py:437
  83.1 2.5 %collective-permute-start.21 = (f32[3,16,128]{2,1,0:T(8,128)S(1)}, f32[3,16,128]{2,1,0:T(8,128)S(1)}, u32[]{:S(2)}, u32[]{:S(2)}) collective-permute-start(f32[3,16,128]{2,1,0:T(8,128)S(1)} %get-tuple-element.51), channel_id=1, source_target_pairs={{0,96},{16,112},{32,0},{48,16},{64,32},{80,48},{96,64},{112,80},{1... | collective-permute-start | bytes 73736 | tf_op jit(solution)/shard_map/ppermute | solution.py:437
  85.7 0.5 collective-permute-done.19.refs_1_
  86.2 0.4 collective-permute-done.20.refs_2_
  86.6 0.7 collective-permute-done.21.refs_3_
  87.3 2.7 %all-to-all-done.3.row_ref = f32[16,3,16,128]{3,2,1,0:T(8,128)S(1)} async-done(((f32[16,3,16,128]{3,2,1,0:T(8,128)}), f32[16,3,16,128]{3,2,1,0:T(8,128)S(1)}, u32[]{:S(2)}, u32[]{:S(2)}) %all-to-all-start.3) | async-done | bytes 393248 | tf_op jit(solution)/shard_map/all_to_all | solution.py:441
  90.0 0.7 last_half_step.1
  (21 shorter events, 0.1 us)
Async XLA Ops:
  3.2 23.2 %all-to-all-start = ((f32[16,7,16,128]{3,2,1,0:T(8,128)}), f32[16,7,16,128]{3,2,1,0:T(8,128)S(1)}, u32[]{:S(2)}, u32[]{:S(2)}) async-start(f32[16,7,16,128]{3,2,1,0:T(8,128)} %get-tuple-element.29), calls=%async_computation | async-start | bytes 1835008 | tf_op jit(solution)/shard_map/all_to_all | solution.py:441
  10.4 6.3 %collective-permute-start.5 = (f32[7,16,128]{2,1,0:T(8,128)}, f32[7,16,128]{2,1,0:T(8,128)S(1)}, u32[]{:S(2)}, u32[]{:S(2)}) collective-permute-start(f32[7,16,128]{2,1,0:T(8,128)} %get-tuple-element.30.refs_4_), channel_id=1, source_target_pairs={{0,96},{16,112},{32,0},{48,16},{64,32},{80,48},{96,64},{112,80},{1... | collective-permute-start | bytes 172040 | tf_op jit(solution)/shard_map/ppermute | solution.py:437
  14.5 5.9 %collective-permute-start.3 = (f32[7,16,128]{2,1,0:T(8,128)}, f32[7,16,128]{2,1,0:T(8,128)S(1)}, u32[]{:S(2)}, u32[]{:S(2)}) collective-permute-start(f32[7,16,128]{2,1,0:T(8,128)} %get-tuple-element.30.refs_4_), channel_id=1, source_target_pairs={{0,64},{16,80},{32,96},{48,112},{64,0},{80,16},{96,32},{112,48},{1... | collective-permute-start | bytes 172040 | tf_op jit(solution)/shard_map/ppermute | solution.py:437
  14.5 6.2 %collective-permute-start.1 = (f32[7,16,128]{2,1,0:T(8,128)}, f32[7,16,128]{2,1,0:T(8,128)S(1)}, u32[]{:S(2)}, u32[]{:S(2)}) collective-permute-start(f32[7,16,128]{2,1,0:T(8,128)} %get-tuple-element.30.refs_4_), channel_id=1, source_target_pairs={{0,32},{16,48},{32,64},{48,80},{64,96},{80,112},{96,0},{112,16},{1... | collective-permute-start | bytes 172040 | tf_op jit(solution)/shard_map/ppermute | solution.py:437
  15.7 5.2 %collective-permute-start = (f32[7,16,128]{2,1,0:T(8,128)}, f32[7,16,128]{2,1,0:T(8,128)S(1)}, u32[]{:S(2)}, u32[]{:S(2)}) collective-permute-start(f32[7,16,128]{2,1,0:T(8,128)} %get-tuple-element.30.refs_4_), channel_id=1, source_target_pairs={{0,16},{16,0},{32,48},{48,32},{64,80},{80,64},{96,112},{112,96},{1... | collective-permute-start | bytes 172040 | tf_op jit(solution)/shard_map/ppermute | solution.py:432
  16.6 4.3 %collective-permute-start.6 = (f32[7,16,128]{2,1,0:T(8,128)S(1)}, f32[7,16,128]{2,1,0:T(8,128)S(1)}, u32[]{:S(2)}, u32[]{:S(2)}) collective-permute-start(f32[7,16,128]{2,1,0:T(8,128)S(1)} %collective-permute-done.5.refs_8_), channel_id=1, source_target_pairs={{0,16},{16,0},{32,48},{48,32},{64,80},{80,64},{96,112},{112,96},{1... | collective-permute-start | bytes 172040 | tf_op jit(solution)/shard_map/ppermute | solution.py:432
  20.4 1.2 %collective-permute-start.4 = (f32[7,16,128]{2,1,0:T(8,128)S(1)}, f32[7,16,128]{2,1,0:T(8,128)S(1)}, u32[]{:S(2)}, u32[]{:S(2)}) collective-permute-start(f32[7,16,128]{2,1,0:T(8,128)S(1)} %collective-permute-done.3.refs_6_), channel_id=1, source_target_pairs={{0,16},{16,0},{32,48},{48,32},{64,80},{80,64},{96,112},{112,96},{1... | collective-permute-start | bytes 172040 | tf_op jit(solution)/shard_map/ppermute | solution.py:432
  20.7 1.2 %collective-permute-start.2 = (f32[7,16,128]{2,1,0:T(8,128)S(1)}, f32[7,16,128]{2,1,0:T(8,128)S(1)}, u32[]{:S(2)}, u32[]{:S(2)}) collective-permute-start(f32[7,16,128]{2,1,0:T(8,128)S(1)} %collective-permute-done.1.refs_4_), channel_id=1, source_target_pairs={{0,16},{16,0},{32,48},{48,32},{64,80},{80,64},{96,112},{112,96},{1... | collective-permute-start | bytes 172040 | tf_op jit(solution)/shard_map/ppermute | solution.py:432
  26.4 0.7 copy-start.3
  27.1 22.4 %copy-start = (f32[7,16,128]{2,1,0:T(8,128)S(1)}, f32[7,16,128]{2,1,0:T(8,128)}, u32[]{:S(2)}) copy-start(f32[7,16,128]{2,1,0:T(8,128)} %get-tuple-element.30.refs_4_) | copy-start | bytes 172036
  27.1 22.4 %copy-start.1 = (f32[3,16,128]{2,1,0:T(8,128)S(1)}, f32[3,16,128]{2,1,0:T(8,128)}, u32[]{:S(2)}) copy-start(f32[3,16,128]{2,1,0:T(8,128)} %get-tuple-element.41.refs_5_) | copy-start | bytes 73732
  27.1 22.4 %copy-start.2 = (f32[3,16,128]{2,1,0:T(8,128)S(1)}, f32[3,16,128]{2,1,0:T(8,128)}, u32[]{:S(2)}) copy-start(f32[3,16,128]{2,1,0:T(8,128)} %get-tuple-element.42.refs_6_) | copy-start | bytes 73732
  27.1 39.7 %copy-start.4 = (f32[5,128]{1,0:T(8,128)S(1)}, f32[5,128]{1,0:T(8,128)}, u32[]{:S(2)}) copy-start(f32[5,128]{1,0:T(8,128)} %get-tuple-element.28.ids_ref) | copy-start | bytes 7684
  33.1 16.4 %all-to-all-start.1 = ((f32[16,3,16,128]{3,2,1,0:T(8,128)}), f32[16,3,16,128]{3,2,1,0:T(8,128)S(1)}, u32[]{:S(2)}, u32[]{:S(2)}) async-start(f32[16,3,16,128]{3,2,1,0:T(8,128)} %bitcast.3), calls=%async_computation.1 | async-start | bytes 786432 | tf_op jit(solution)/shard_map/all_to_all | solution.py:441
  37.8 1.4 %collective-permute-start.7 = (f32[4,3,16,128]{3,2,1,0:T(8,128)S(1)}, f32[4,3,16,128]{3,2,1,0:T(8,128)S(1)}, u32[]{:S(2)}, u32[]{:S(2)}) collective-permute-start(f32[4,3,16,128]{3,2,1,0:T(8,128)S(1)} %get-tuple-element.36), channel_id=1, source_target_pairs={{0,16},{16,0},{32,48},{48,32},{64,80},{80,64},{96,112},{112,96},{1... | collective-permute-start | bytes 294920 | tf_op jit(solution)/shard_map/ppermute | solution.py:432
  39.2 7.3 %collective-permute-start.8 = (f32[3,16,128]{2,1,0:T(8,128)S(1)}, f32[3,16,128]{2,1,0:T(8,128)S(1)}, u32[]{:S(2)}, u32[]{:S(2)}) collective-permute-start(f32[3,16,128]{2,1,0:T(8,128)S(1)} %get-tuple-element.38), channel_id=1, source_target_pairs={{0,32},{16,48},{32,64},{48,80},{64,96},{80,112},{96,0},{112,16},{1... | collective-permute-start | bytes 73736 | tf_op jit(solution)/shard_map/ppermute | solution.py:437
  42.1 5.6 %collective-permute-start.9 = (f32[3,16,128]{2,1,0:T(8,128)S(1)}, f32[3,16,128]{2,1,0:T(8,128)S(1)}, u32[]{:S(2)}, u32[]{:S(2)}) collective-permute-start(f32[3,16,128]{2,1,0:T(8,128)S(1)} %get-tuple-element.39), channel_id=1, source_target_pairs={{0,64},{16,80},{32,96},{48,112},{64,0},{80,16},{96,32},{112,48},{1... | collective-permute-start | bytes 73736 | tf_op jit(solution)/shard_map/ppermute | solution.py:437
  45.6 3.8 %collective-permute-start.10 = (f32[3,16,128]{2,1,0:T(8,128)S(1)}, f32[3,16,128]{2,1,0:T(8,128)S(1)}, u32[]{:S(2)}, u32[]{:S(2)}) collective-permute-start(f32[3,16,128]{2,1,0:T(8,128)S(1)} %get-tuple-element.40), channel_id=1, source_target_pairs={{0,96},{16,112},{32,0},{48,16},{64,32},{80,48},{96,64},{112,80},{1... | collective-permute-start | bytes 73736 | tf_op jit(solution)/shard_map/ppermute | solution.py:437
  50.3 16.5 %all-to-all-start.2 = ((f32[16,3,16,128]{3,2,1,0:T(8,128)}), f32[16,3,16,128]{3,2,1,0:T(8,128)S(1)}, u32[]{:S(2)}, u32[]{:S(2)}) async-start(f32[16,3,16,128]{3,2,1,0:T(8,128)} %get-tuple-element.43), calls=%async_computation.2 | async-start | bytes 786432 | tf_op jit(solution)/shard_map/all_to_all | solution.py:441
  57.4 3.9 %collective-permute-start.16 = (f32[3,16,128]{2,1,0:T(8,128)S(1)}, f32[3,16,128]{2,1,0:T(8,128)S(1)}, u32[]{:S(2)}, u32[]{:S(2)}) collective-permute-start(f32[3,16,128]{2,1,0:T(8,128)S(1)} %get-tuple-element.44), channel_id=1, source_target_pairs={{0,96},{16,112},{32,0},{48,16},{64,32},{80,48},{96,64},{112,80},{1... | collective-permute-start | bytes 73736 | tf_op jit(solution)/shard_map/ppermute | solution.py:437
  59.4 5.3 %collective-permute-start.14 = (f32[3,16,128]{2,1,0:T(8,128)S(1)}, f32[3,16,128]{2,1,0:T(8,128)S(1)}, u32[]{:S(2)}, u32[]{:S(2)}) collective-permute-start(f32[3,16,128]{2,1,0:T(8,128)S(1)} %get-tuple-element.44), channel_id=1, source_target_pairs={{0,64},{16,80},{32,96},{48,112},{64,0},{80,16},{96,32},{112,48},{1... | collective-permute-start | bytes 73736 | tf_op jit(solution)/shard_map/ppermute | solution.py:437
  59.4 5.3 %collective-permute-start.12 = (f32[3,16,128]{2,1,0:T(8,128)S(1)}, f32[3,16,128]{2,1,0:T(8,128)S(1)}, u32[]{:S(2)}, u32[]{:S(2)}) collective-permute-start(f32[3,16,128]{2,1,0:T(8,128)S(1)} %get-tuple-element.44), channel_id=1, source_target_pairs={{0,32},{16,48},{32,64},{48,80},{64,96},{80,112},{96,0},{112,16},{1... | collective-permute-start | bytes 73736 | tf_op jit(solution)/shard_map/ppermute | solution.py:437
  60.4 4.8 %collective-permute-start.11 = (f32[3,16,128]{2,1,0:T(8,128)S(1)}, f32[3,16,128]{2,1,0:T(8,128)S(1)}, u32[]{:S(2)}, u32[]{:S(2)}) collective-permute-start(f32[3,16,128]{2,1,0:T(8,128)S(1)} %get-tuple-element.44), channel_id=1, source_target_pairs={{0,16},{16,0},{32,48},{48,32},{64,80},{80,64},{96,112},{112,96},{1... | collective-permute-start | bytes 73736 | tf_op jit(solution)/shard_map/ppermute | solution.py:432
  61.3 3.9 %collective-permute-start.17 = (f32[3,16,128]{2,1,0:T(8,128)S(1)}, f32[3,16,128]{2,1,0:T(8,128)S(1)}, u32[]{:S(2)}, u32[]{:S(2)}) collective-permute-start(f32[3,16,128]{2,1,0:T(8,128)S(1)} %collective-permute-done.16.refs_9_), channel_id=1, source_target_pairs={{0,16},{16,0},{32,48},{48,32},{64,80},{80,64},{96,112},{112,96},{1... | collective-permute-start | bytes 73736 | tf_op jit(solution)/shard_map/ppermute | solution.py:432
  64.7 1.2 %collective-permute-start.15 = (f32[3,16,128]{2,1,0:T(8,128)S(1)}, f32[3,16,128]{2,1,0:T(8,128)S(1)}, u32[]{:S(2)}, u32[]{:S(2)}) collective-permute-start(f32[3,16,128]{2,1,0:T(8,128)S(1)} %collective-permute-done.14.refs_7_), channel_id=1, source_target_pairs={{0,16},{16,0},{32,48},{48,32},{64,80},{80,64},{96,112},{112,96},{1... | collective-permute-start | bytes 73736 | tf_op jit(solution)/shard_map/ppermute | solution.py:432
  64.7 1.4 %collective-permute-start.13 = (f32[3,16,128]{2,1,0:T(8,128)S(1)}, f32[3,16,128]{2,1,0:T(8,128)S(1)}, u32[]{:S(2)}, u32[]{:S(2)}) collective-permute-start(f32[3,16,128]{2,1,0:T(8,128)S(1)} %collective-permute-done.12.refs_5_), channel_id=1, source_target_pairs={{0,16},{16,0},{32,48},{48,32},{64,80},{80,64},{96,112},{112,96},{1... | collective-permute-start | bytes 73736 | tf_op jit(solution)/shard_map/ppermute | solution.py:432
  71.5 18.6 %all-to-all-start.3 = ((f32[16,3,16,128]{3,2,1,0:T(8,128)}), f32[16,3,16,128]{3,2,1,0:T(8,128)S(1)}, u32[]{:S(2)}, u32[]{:S(2)}) async-start(f32[16,3,16,128]{3,2,1,0:T(8,128)} %bitcast.4), calls=%async_computation.3 | async-start | bytes 786432 | tf_op jit(solution)/shard_map/all_to_all | solution.py:441
  79.7 1.4 %collective-permute-start.18 = (f32[4,3,16,128]{3,2,1,0:T(8,128)S(1)}, f32[4,3,16,128]{3,2,1,0:T(8,128)S(1)}, u32[]{:S(2)}, u32[]{:S(2)}) collective-permute-start(f32[4,3,16,128]{3,2,1,0:T(8,128)S(1)} %get-tuple-element.47), channel_id=1, source_target_pairs={{0,16},{16,0},{32,48},{48,32},{64,80},{80,64},{96,112},{112,96},{1... | collective-permute-start | bytes 294920 | tf_op jit(solution)/shard_map/ppermute | solution.py:432
  81.1 5.1 %collective-permute-start.19 = (f32[3,16,128]{2,1,0:T(8,128)S(1)}, f32[3,16,128]{2,1,0:T(8,128)S(1)}, u32[]{:S(2)}, u32[]{:S(2)}) collective-permute-start(f32[3,16,128]{2,1,0:T(8,128)S(1)} %get-tuple-element.49), channel_id=1, source_target_pairs={{0,32},{16,48},{32,64},{48,80},{64,96},{80,112},{96,0},{112,16},{1... | collective-permute-start | bytes 73736 | tf_op jit(solution)/shard_map/ppermute | solution.py:437
  81.2 5.4 %collective-permute-start.20 = (f32[3,16,128]{2,1,0:T(8,128)S(1)}, f32[3,16,128]{2,1,0:T(8,128)S(1)}, u32[]{:S(2)}, u32[]{:S(2)}) collective-permute-start(f32[3,16,128]{2,1,0:T(8,128)S(1)} %get-tuple-element.50), channel_id=1, source_target_pairs={{0,64},{16,80},{32,96},{48,112},{64,0},{80,16},{96,32},{112,48},{1... | collective-permute-start | bytes 73736 | tf_op jit(solution)/shard_map/ppermute | solution.py:437
  83.1 4.2 %collective-permute-start.21 = (f32[3,16,128]{2,1,0:T(8,128)S(1)}, f32[3,16,128]{2,1,0:T(8,128)S(1)}, u32[]{:S(2)}, u32[]{:S(2)}) collective-permute-start(f32[3,16,128]{2,1,0:T(8,128)S(1)} %get-tuple-element.51), channel_id=1, source_target_pairs={{0,96},{16,112},{32,0},{48,16},{64,32},{80,48},{96,64},{112,80},{1... | collective-permute-start | bytes 73736 | tf_op jit(solution)/shard_map/ppermute | solution.py:437
where the time goes:
time: 90.7 us
  starting transfers between devices  48.3 us (53%)
  waiting for transfers between devices  26.2 us (29%)
  Pallas kernels  14.1 us (16%)
  between operations  1.39 us (2%)
    all_to_all x4, starting transfers between devices, swap(): return lax.all_to_all(x, 'col', 0, 0, tiled=True)  27.1 us
    ppermute x12, starting transfers between devices, along_z(): lax.ppermute(x, 'row', [(i, (i // CORES + d) % n_z * CORES + i % CORES) f...  20.2 us
    ppermute x12, waiting for transfers between devices, along_z(): lax.ppermute(x, 'row', [(i, (i // CORES + d) % n_z * CORES + i % CORES) f...  13.8 us
    pallas_call x2, Pallas kernels, pair_forces(): pl.pallas_call(functools.partial(pair_kernel, n_row, fresh), out_shape=ou...  10.6 us
    all_to_all x4, waiting for transfers between devices, swap(): return lax.all_to_all(x, 'col', 0, 0, tiled=True)  7.94 us
    ppermute x10, waiting for transfers between devices, to_sibling(): return lax.ppermute(x, 'row', [(i, i ^ 1) for i in range(n_row)])  4.42 us
    pallas_call x1, Pallas kernels, start(): pl.pallas_call(start_kernel, out_shape=(f32(n_col, 7, TILE_DEV, TILE), f3...  1.96 us
  transfers between devices with their start and end apart: 26, of which 19 were waited for; matrix products, arithmetic and copies ran while one was open for 0% of the time, Pallas kernels for 0%

commit v1 on v0

--- a/solution.py
+++ b/solution.py
@@ -16,7 +16,7 @@
 CENTRE = 2.0
 STRENGTH = 1.5 / math.sqrt(TILE * (1.0 + PAIRS_DEV / TILE_DEV))
 UNROLL = 16
-LEAD = 4
+LEAD = 5
 CORES = 2
 LIMIT = 50 * 2**20
 SMALL = 4 * 2**20
@@ -127,6 +127,26 @@
     z, core = at_row // CORES, at_row % CORES
     fetch = pltpu.make_async_copy(ids_ref, list_ref, list_sem)
     fetch.start()
+
+    def copies(i):
+        part = pl.ds(i * UNROLL, UNROLL)
+        if not fresh:
+            return (pltpu.make_async_copy(all_stiff_ref.at[part], stiff_ref.at[part], sems.at[0, i]),)
+        return (
+            pltpu.make_async_copy(bond_ref.at[part], bonds_ref.at[part], sems.at[0, i]),
+            pltpu.make_async_copy(broken_ref.at[part], cracks_ref.at[part], sems.at[1, i]),
+        )
+
+    def store(i):
+        part = pl.ds(i * UNROLL, UNROLL)
+        return pltpu.make_async_copy(stiff_ref.at[part], all_stiff_ref.at[part], out_sems.at[i])
+
+    def begin(i, carry):
+        for copy in copies(i):
+            copy.start()
+        return carry
+
+    begin(0, 0)
     if fresh:
         states = (
             pltpu.make_async_copy(rows_ref, all_rows_ref, state_sems.at[0]),
@@ -145,25 +165,7 @@
     live = list_ref[2, 0].astype(jnp.int32)
     chunks = (live + UNROLL - 1) // UNROLL
 
-    def copies(i):
-        part = pl.ds(i * UNROLL, UNROLL)
-        if not fresh:
-            return (pltpu.make_async_copy(all_stiff_ref.at[part], stiff_ref.at[part], sems.at[0, i]),)
-        return (
-            pltpu.make_async_copy(bond_ref.at[part], bonds_ref.at[part], sems.at[0, i]),
-            pltpu.make_async_copy(broken_ref.at[part], cracks_ref.at[part], sems.at[1, i]),
-        )
-
-    def store(i):
-        part = pl.ds(i * UNROLL, UNROLL)
-        return pltpu.make_async_copy(stiff_ref.at[part], all_stiff_ref.at[part], out_sems.at[i])
-
-    def begin(i, carry):
-        for copy in copies(i):
-            copy.start()
-        return carry
-
-    lax.fori_loop(0, chunks, begin, 0)
+    lax.fori_loop(1, chunks, begin, 0)
     rowf_ref[...] = jnp.zeros_like(rowf_ref)
     colf_ref[...] = jnp.zeros_like(colf_ref)
     if not fresh:

time: 90.7 us -> 92.3 us (1.018); the launches traced: 90.7 us -> 91.1 us
  no operation moved by 1% of the time
where the time goes in v1:
time: 92.3 us; the launch traced here: 91.1 us
  starting transfers between devices  49.1 us (53%)
  waiting for transfers between devices  26.2 us (28%)
  Pallas kernels  13.7 us (15%)
  between operations  1.38 us (1%)
    all_to_all x4, starting transfers between devices, swap(): return lax.all_to_all(x, 'col', 0, 0, tiled=True)  26.9 us
    ppermute x12, starting transfers between devices, along_z(): lax.ppermute(x, 'row', [(i, (i // CORES + d) % n_z * CORES + i % CORES) f...  20.9 us
    ppermute x12, waiting for transfers between devices, along_z(): lax.ppermute(x, 'row', [(i, (i // CORES + d) % n_z * CORES + i % CORES) f...  14.7 us
    pallas_call x2, Pallas kernels, pair_forces(): pl.pallas_call(functools.partial(pair_kernel, n_row, fresh), out_shape=ou...  10.2 us
    all_to_all x4, waiting for transfers between devices, swap(): return lax.all_to_all(x, 'col', 0, 0, tiled=True)  7.42 us
    ppermute x10, waiting for transfers between devices, to_sibling(): return lax.ppermute(x, 'row', [(i, i ^ 1) for i in range(n_row)])  4 us
    pallas_call x1, Pallas kernels, start(): pl.pallas_call(start_kernel, out_shape=(f32(n_col, 7, TILE_DEV, TILE), f3...  1.96 us
  transfers between devices with their start and end apart: 26, of which 19 were waited for; matrix products, arithmetic and copies ran while one was open for 0% of the time, Pallas kernels for 0%

profile of v1, /device:TPU:0, one launch (start us, length us, event | category | flops | bytes accessed | tf_op | source)
XLA Modules:
  0.0 91.1 jit_solution(1994643197115847590)
XLA Ops:
  1.3 2.0 %first_half_step.1 = (f32[16,7,16,128]{3,2,1,0:T(8,128)}, f32[7,16,128]{2,1,0:T(8,128)}, f32[3,16,128]{2,1,0:T(8,128)}, f32[3,16,128]{2,1,0:T(8,128)}, f32[5,128]{1,0:T(8,128)}) custom-call(f32[2]{0:T(128)} %moduli_ref.1, s32[1]{0:T(128)S(6)} %copy.13.count_ref, s32[1,128]{1,0:T(1,128)} %bitcast.6, s32[1,128]{1,0:T(1,128)} %bitcast.7, s32[16,128]{1,0:T(8,128)} %bitcast.5, ...), custom_call_target="tpu_custom_call" | custom-call | tf_op jit(solution)/shard_map/first_half_step/pallas_call | solution.py:346
  3.2 7.1 %all-to-all-start = ((f32[16,7,16,128]{3,2,1,0:T(8,128)}), f32[16,7,16,128]{3,2,1,0:T(8,128)S(1)}, u32[]{:S(2)}, u32[]{:S(2)}) async-start(f32[16,7,16,128]{3,2,1,0:T(8,128)} %get-tuple-element.29), calls=%async_computation | async-start | bytes 1835008 | tf_op jit(solution)/shard_map/all_to_all | solution.py:443
  10.4 4.1 %collective-permute-start.5 = (f32[7,16,128]{2,1,0:T(8,128)}, f32[7,16,128]{2,1,0:T(8,128)S(1)}, u32[]{:S(2)}, u32[]{:S(2)}) collective-permute-start(f32[7,16,128]{2,1,0:T(8,128)} %get-tuple-element.30.refs_4_), channel_id=1, source_target_pairs={{0,96},{16,112},{32,0},{48,16},{64,32},{80,48},{96,64},{112,80},{1... | collective-permute-start | bytes 172040 | tf_op jit(solution)/shard_map/ppermute | solution.py:439
  14.5 0.0 collective-permute-start.3
  14.5 1.3 %collective-permute-start.1 = (f32[7,16,128]{2,1,0:T(8,128)}, f32[7,16,128]{2,1,0:T(8,128)S(1)}, u32[]{:S(2)}, u32[]{:S(2)}) collective-permute-start(f32[7,16,128]{2,1,0:T(8,128)} %get-tuple-element.30.refs_4_), channel_id=1, source_target_pairs={{0,32},{16,48},{32,64},{48,80},{64,96},{80,112},{96,0},{112,16},{1... | collective-permute-start | bytes 172040 | tf_op jit(solution)/shard_map/ppermute | solution.py:439
  15.7 0.9 collective-permute-done.5.refs_8_
  16.6 0.0 collective-permute-start.6
  16.6 3.8 %collective-permute-done.3.refs_6_ = f32[7,16,128]{2,1,0:T(8,128)S(1)} collective-permute-done((f32[7,16,128]{2,1,0:T(8,128)}, f32[7,16,128]{2,1,0:T(8,128)S(1)}, u32[]{:S(2)}, u32[]{:S(2)}) %collective-permute-start.3) | collective-permute-done | bytes 57376 | tf_op jit(solution)/shard_map/ppermute | solution.py:439
  20.4 0.3 collective-permute-done.1.refs_4_
  20.7 0.2 collective-permute-start.2
  20.9 0.7 collective-permute-done.4.refs_7_
  21.7 0.3 collective-permute-done.2.refs_5_
  21.9 4.5 %all-to-all-done.refs_2_ = f32[16,7,16,128]{3,2,1,0:T(8,128)S(1)} async-done(((f32[16,7,16,128]{3,2,1,0:T(8,128)}), f32[16,7,16,128]{3,2,1,0:T(8,128)S(1)}, u32[]{:S(2)}, u32[]{:S(2)}) %all-to-all-start) | async-done | bytes 917536 | tf_op jit(solution)/shard_map/all_to_all | solution.py:443
  26.4 0.7 copy-done.3
  27.1 5.7 %pair_forces.1 = (f32[768,128]{1,0:T(8,128)}, f32[4,3,16,128]{3,2,1,0:T(8,128)S(1)}, f32[4,3,16,128]{3,2,1,0:T(8,128)S(1)}, f32[2048,128]{1,0:T(8,128)S(1)}, f32...) custom-call(f32[5,128]{1,0:T(8,128)S(1)} %copy-done.3, s32[128,128,128]{2,1,0:T(8,128)} %refs_0_.1, ...), custom_call_target="tpu_custom_call" | custom-call | tf_op jit(solution)/shard_map/pair_forces/pallas_call | solution.py:297
  32.9 4.7 %all-to-all-start.1 = ((f32[16,3,16,128]{3,2,1,0:T(8,128)}), f32[16,3,16,128]{3,2,1,0:T(8,128)S(1)}, u32[]{:S(2)}, u32[]{:S(2)}) async-start(f32[16,3,16,128]{3,2,1,0:T(8,128)} %bitcast.3), calls=%async_computation.1 | async-start | bytes 786432 | tf_op jit(solution)/shard_map/all_to_all | solution.py:443
  37.6 0.2 collective-permute-start.7
  37.7 1.2 %collective-permute-done.7.other_ref = f32[4,3,16,128]{3,2,1,0:T(8,128)S(1)} collective-permute-done((f32[4,3,16,128]{3,2,1,0:T(8,128)S(1)}, f32[4,3,16,128]{3,2,1,0:T(8,128)S(1)}, u32[]{:S(2)}, u32[]{:S(2)}) %collective-permute-start.7) | collective-permute-done | bytes 98336 | tf_op jit(solution)/shard_map/ppermute | solution.py:434
  39.0 2.9 %collective-permute-start.8 = (f32[3,16,128]{2,1,0:T(8,128)S(1)}, f32[3,16,128]{2,1,0:T(8,128)S(1)}, u32[]{:S(2)}, u32[]{:S(2)}) collective-permute-start(f32[3,16,128]{2,1,0:T(8,128)S(1)} %get-tuple-element.38), channel_id=1, source_target_pairs={{0,32},{16,48},{32,64},{48,80},{64,96},{80,112},{96,0},{112,16},{1... | collective-permute-start | bytes 73736 | tf_op jit(solution)/shard_map/ppermute | solution.py:439
  41.9 3.9 %collective-permute-start.9 = (f32[3,16,128]{2,1,0:T(8,128)S(1)}, f32[3,16,128]{2,1,0:T(8,128)S(1)}, u32[]{:S(2)}, u32[]{:S(2)}) collective-permute-start(f32[3,16,128]{2,1,0:T(8,128)S(1)} %get-tuple-element.39), channel_id=1, source_target_pairs={{0,64},{16,80},{32,96},{48,112},{64,0},{80,16},{96,32},{112,48},{1... | collective-permute-start | bytes 73736 | tf_op jit(solution)/shard_map/ppermute | solution.py:439
  45.8 0.7 collective-permute-start.10
  46.5 0.0 collective-permute-done.8.refs_1_
  46.5 1.4 %collective-permute-done.9.refs_2_ = f32[3,16,128]{2,1,0:T(8,128)S(1)} collective-permute-done((f32[3,16,128]{2,1,0:T(8,128)S(1)}, f32[3,16,128]{2,1,0:T(8,128)S(1)}, u32[]{:S(2)}, u32[]{:S(2)}) %collective-permute-start.9) | collective-permute-done | bytes 24608 | tf_op jit(solution)/shard_map/ppermute | solution.py:439
  47.9 1.8 %collective-permute-done.10.refs_3_ = f32[3,16,128]{2,1,0:T(8,128)S(1)} collective-permute-done((f32[3,16,128]{2,1,0:T(8,128)S(1)}, f32[3,16,128]{2,1,0:T(8,128)S(1)}, u32[]{:S(2)}, u32[]{:S(2)}) %collective-permute-start.10) | collective-permute-done | bytes 24608 | tf_op jit(solution)/shard_map/ppermute | solution.py:439
  49.6 0.0 all-to-all-done.1.row_ref
  49.6 0.9 next_step.1
  50.5 6.9 %all-to-all-start.2 = ((f32[16,3,16,128]{3,2,1,0:T(8,128)}), f32[16,3,16,128]{3,2,1,0:T(8,128)S(1)}, u32[]{:S(2)}, u32[]{:S(2)}) async-start(f32[16,3,16,128]{3,2,1,0:T(8,128)} %get-tuple-element.43), calls=%async_computation.2 | async-start | bytes 786432 | tf_op jit(solution)/shard_map/all_to_all | solution.py:443
  57.4 2.2 %collective-permute-start.16 = (f32[3,16,128]{2,1,0:T(8,128)S(1)}, f32[3,16,128]{2,1,0:T(8,128)S(1)}, u32[]{:S(2)}, u32[]{:S(2)}) collective-permute-start(f32[3,16,128]{2,1,0:T(8,128)S(1)} %get-tuple-element.44), channel_id=1, source_target_pairs={{0,96},{16,112},{32,0},{48,16},{64,32},{80,48},{96,64},{112,80},{1... | collective-permute-start | bytes 73736 | tf_op jit(solution)/shard_map/ppermute | solution.py:439
  59.6 0.9 %collective-permute-start.12 = (f32[3,16,128]{2,1,0:T(8,128)S(1)}, f32[3,16,128]{2,1,0:T(8,128)S(1)}, u32[]{:S(2)}, u32[]{:S(2)}) collective-permute-start(f32[3,16,128]{2,1,0:T(8,128)S(1)} %get-tuple-element.44), channel_id=1, source_target_pairs={{0,32},{16,48},{32,64},{48,80},{64,96},{80,112},{96,0},{112,16},{1... | collective-permute-start | bytes 73736 | tf_op jit(solution)/shard_map/ppermute | solution.py:439
  60.5 0.0 collective-permute-start.11
  60.5 0.8 collective-permute-done.16.refs_9_
  61.3 3.6 %collective-permute-done.14.refs_7_ = f32[3,16,128]{2,1,0:T(8,128)S(1)} collective-permute-done((f32[3,16,128]{2,1,0:T(8,128)S(1)}, f32[3,16,128]{2,1,0:T(8,128)S(1)}, u32[]{:S(2)}, u32[]{:S(2)}) %collective-permute-start.14) | collective-permute-done | bytes 24608 | tf_op jit(solution)/shard_map/ppermute | solution.py:439
  64.9 0.5 collective-permute-start.13
  65.4 0.7 collective-permute-done.15.refs_8_
  66.1 0.2 collective-permute-done.13.refs_6_
  66.3 0.5 all-to-all-done.2.refs_3_
  66.8 4.4 %pair_forces_again.1 = (f32[768,128]{1,0:T(8,128)}, f32[4,3,16,128]{3,2,1,0:T(8,128)S(1)}, f32[4,3,16,128]{3,2,1,0:T(8,128)S(1)}) custom-call(f32[5,128]{1,0:T(8,128)S(1)} %copy-done.4, f32[2048,128]{1,0:T(8,128)S(1)} %get-tuple-element.31.refs_0_, f32[1024,128]{1,0:T(8,128)S(1)} %get-tuple-element.32.refs_1_, f32[128,128,128]{2,1,0:T(8,128)} %get-tuple-element.33.refs_2_, ...), custom_call_target="tpu_custom_call" | custom-call | tf_op jit(solution)/shard_map/pair_forces_again/pallas_call | solution.py:297
  71.2 8.2 %all-to-all-start.3 = ((f32[16,3,16,128]{3,2,1,0:T(8,128)}), f32[16,3,16,128]{3,2,1,0:T(8,128)S(1)}, u32[]{:S(2)}, u32[]{:S(2)}) async-start(f32[16,3,16,128]{3,2,1,0:T(8,128)} %bitcast.4), calls=%async_computation.3 | async-start | bytes 786432 | tf_op jit(solution)/shard_map/all_to_all | solution.py:443
  79.4 0.4 collective-permute-start.18
  79.9 0.9 %collective-permute-done.18.other_ref = f32[4,3,16,128]{3,2,1,0:T(8,128)S(1)} collective-permute-done((f32[4,3,16,128]{3,2,1,0:T(8,128)S(1)}, f32[4,3,16,128]{3,2,1,0:T(8,128)S(1)}, u32[]{:S(2)}, u32[]{:S(2)}) %collective-permute-start.18) | collective-permute-done | bytes 98336 | tf_op jit(solution)/shard_map/ppermute | solution.py:434
  80.9 0.1 collective-permute-start.19
  80.9 3.2 %collective-permute-start.20 = (f32[3,16,128]{2,1,0:T(8,128)S(1)}, f32[3,16,128]{2,1,0:T(8,128)S(1)}, u32[]{:S(2)}, u32[]{:S(2)}) collective-permute-start(f32[3,16,128]{2,1,0:T(8,128)S(1)} %get-tuple-element.50), channel_id=1, source_target_pairs={{0,64},{16,80},{32,96},{48,112},{64,0},{80,16},{96,32},{112,48},{1... | collective-permute-start | bytes 73736 | tf_op jit(solution)/shard_map/ppermute | solution.py:439
  84.1 1.5 %collective-permute-start.21 = (f32[3,16,128]{2,1,0:T(8,128)S(1)}, f32[3,16,128]{2,1,0:T(8,128)S(1)}, u32[]{:S(2)}, u32[]{:S(2)}) collective-permute-start(f32[3,16,128]{2,1,0:T(8,128)S(1)} %get-tuple-element.51), channel_id=1, source_target_pairs={{0,96},{16,112},{32,0},{48,16},{64,32},{80,48},{96,64},{112,80},{1... | collective-permute-start | bytes 73736 | tf_op jit(solution)/shard_map/ppermute | solution.py:439
  85.7 0.3 collective-permute-done.19.refs_1_
  86.0 0.3 collective-permute-done.20.refs_2_
  86.4 1.6 %collective-permute-done.21.refs_3_ = f32[3,16,128]{2,1,0:T(8,128)S(1)} collective-permute-done((f32[3,16,128]{2,1,0:T(8,128)S(1)}, f32[3,16,128]{2,1,0:T(8,128)S(1)}, u32[]{:S(2)}, u32[]{:S(2)}) %collective-permute-start.21) | collective-permute-done | bytes 24608 | tf_op jit(solution)/shard_map/ppermute | solution.py:439
  88.0 2.4 %all-to-all-done.3.row_ref = f32[16,3,16,128]{3,2,1,0:T(8,128)S(1)} async-done(((f32[16,3,16,128]{3,2,1,0:T(8,128)}), f32[16,3,16,128]{3,2,1,0:T(8,128)S(1)}, u32[]{:S(2)}, u32[]{:S(2)}) %all-to-all-start.3) | async-done | bytes 393248 | tf_op jit(solution)/shard_map/all_to_all | solution.py:443
  90.4 0.7 last_half_step.1
  (21 shorter events, 0.1 us)
Async XLA Ops:
  3.2 23.2 %all-to-all-start = ((f32[16,7,16,128]{3,2,1,0:T(8,128)}), f32[16,7,16,128]{3,2,1,0:T(8,128)S(1)}, u32[]{:S(2)}, u32[]{:S(2)}) async-start(f32[16,7,16,128]{3,2,1,0:T(8,128)} %get-tuple-element.29), calls=%async_computation | async-start | bytes 1835008 | tf_op jit(solution)/shard_map/all_to_all | solution.py:443
  10.4 6.3 %collective-permute-start.5 = (f32[7,16,128]{2,1,0:T(8,128)}, f32[7,16,128]{2,1,0:T(8,128)S(1)}, u32[]{:S(2)}, u32[]{:S(2)}) collective-permute-start(f32[7,16,128]{2,1,0:T(8,128)} %get-tuple-element.30.refs_4_), channel_id=1, source_target_pairs={{0,96},{16,112},{32,0},{48,16},{64,32},{80,48},{96,64},{112,80},{1... | collective-permute-start | bytes 172040 | tf_op jit(solution)/shard_map/ppermute | solution.py:439
  14.5 5.9 %collective-permute-start.3 = (f32[7,16,128]{2,1,0:T(8,128)}, f32[7,16,128]{2,1,0:T(8,128)S(1)}, u32[]{:S(2)}, u32[]{:S(2)}) collective-permute-start(f32[7,16,128]{2,1,0:T(8,128)} %get-tuple-element.30.refs_4_), channel_id=1, source_target_pairs={{0,64},{16,80},{32,96},{48,112},{64,0},{80,16},{96,32},{112,48},{1... | collective-permute-start | bytes 172040 | tf_op jit(solution)/shard_map/ppermute | solution.py:439
  14.5 6.2 %collective-permute-start.1 = (f32[7,16,128]{2,1,0:T(8,128)}, f32[7,16,128]{2,1,0:T(8,128)S(1)}, u32[]{:S(2)}, u32[]{:S(2)}) collective-permute-start(f32[7,16,128]{2,1,0:T(8,128)} %get-tuple-element.30.refs_4_), channel_id=1, source_target_pairs={{0,32},{16,48},{32,64},{48,80},{64,96},{80,112},{96,0},{112,16},{1... | collective-permute-start | bytes 172040 | tf_op jit(solution)/shard_map/ppermute | solution.py:439
  15.7 5.2 %collective-permute-start = (f32[7,16,128]{2,1,0:T(8,128)}, f32[7,16,128]{2,1,0:T(8,128)S(1)}, u32[]{:S(2)}, u32[]{:S(2)}) collective-permute-start(f32[7,16,128]{2,1,0:T(8,128)} %get-tuple-element.30.refs_4_), channel_id=1, source_target_pairs={{0,16},{16,0},{32,48},{48,32},{64,80},{80,64},{96,112},{112,96},{1... | collective-permute-start | bytes 172040 | tf_op jit(solution)/shard_map/ppermute | solution.py:434
  16.6 4.3 %collective-permute-start.6 = (f32[7,16,128]{2,1,0:T(8,128)S(1)}, f32[7,16,128]{2,1,0:T(8,128)S(1)}, u32[]{:S(2)}, u32[]{:S(2)}) collective-permute-start(f32[7,16,128]{2,1,0:T(8,128)S(1)} %collective-permute-done.5.refs_8_), channel_id=1, source_target_pairs={{0,16},{16,0},{32,48},{48,32},{64,80},{80,64},{96,112},{112,96},{1... | collective-permute-start | bytes 172040 | tf_op jit(solution)/shard_map/ppermute | solution.py:434
  20.4 1.2 %collective-permute-start.4 = (f32[7,16,128]{2,1,0:T(8,128)S(1)}, f32[7,16,128]{2,1,0:T(8,128)S(1)}, u32[]{:S(2)}, u32[]{:S(2)}) collective-permute-start(f32[7,16,128]{2,1,0:T(8,128)S(1)} %collective-permute-done.3.refs_6_), channel_id=1, source_target_pairs={{0,16},{16,0},{32,48},{48,32},{64,80},{80,64},{96,112},{112,96},{1... | collective-permute-start | bytes 172040 | tf_op jit(solution)/shard_map/ppermute | solution.py:434
  20.7 1.2 %collective-permute-start.2 = (f32[7,16,128]{2,1,0:T(8,128)S(1)}, f32[7,16,128]{2,1,0:T(8,128)S(1)}, u32[]{:S(2)}, u32[]{:S(2)}) collective-permute-start(f32[7,16,128]{2,1,0:T(8,128)S(1)} %collective-permute-done.1.refs_4_), channel_id=1, source_target_pairs={{0,16},{16,0},{32,48},{48,32},{64,80},{80,64},{96,112},{112,96},{1... | collective-permute-start | bytes 172040 | tf_op jit(solution)/shard_map/ppermute | solution.py:434
  26.4 0.7 copy-start.3
  27.1 22.5 %copy-start = (f32[7,16,128]{2,1,0:T(8,128)S(1)}, f32[7,16,128]{2,1,0:T(8,128)}, u32[]{:S(2)}) copy-start(f32[7,16,128]{2,1,0:T(8,128)} %get-tuple-element.30.refs_4_) | copy-start | bytes 172036
  27.1 22.5 %copy-start.1 = (f32[3,16,128]{2,1,0:T(8,128)S(1)}, f32[3,16,128]{2,1,0:T(8,128)}, u32[]{:S(2)}) copy-start(f32[3,16,128]{2,1,0:T(8,128)} %get-tuple-element.41.refs_5_) | copy-start | bytes 73732
  27.1 22.5 %copy-start.2 = (f32[3,16,128]{2,1,0:T(8,128)S(1)}, f32[3,16,128]{2,1,0:T(8,128)}, u32[]{:S(2)}) copy-start(f32[3,16,128]{2,1,0:T(8,128)} %get-tuple-element.42.refs_6_) | copy-start | bytes 73732
  27.1 39.7 %copy-start.4 = (f32[5,128]{1,0:T(8,128)S(1)}, f32[5,128]{1,0:T(8,128)}, u32[]{:S(2)}) copy-start(f32[5,128]{1,0:T(8,128)} %get-tuple-element.28.ids_ref) | copy-start | bytes 7684
  32.9 16.8 %all-to-all-start.1 = ((f32[16,3,16,128]{3,2,1,0:T(8,128)}), f32[16,3,16,128]{3,2,1,0:T(8,128)S(1)}, u32[]{:S(2)}, u32[]{:S(2)}) async-start(f32[16,3,16,128]{3,2,1,0:T(8,128)} %bitcast.3), calls=%async_computation.1 | async-start | bytes 786432 | tf_op jit(solution)/shard_map/all_to_all | solution.py:443
  37.6 1.4 %collective-permute-start.7 = (f32[4,3,16,128]{3,2,1,0:T(8,128)S(1)}, f32[4,3,16,128]{3,2,1,0:T(8,128)S(1)}, u32[]{:S(2)}, u32[]{:S(2)}) collective-permute-start(f32[4,3,16,128]{3,2,1,0:T(8,128)S(1)} %get-tuple-element.36), channel_id=1, source_target_pairs={{0,16},{16,0},{32,48},{48,32},{64,80},{80,64},{96,112},{112,96},{1... | collective-permute-start | bytes 294920 | tf_op jit(solution)/shard_map/ppermute | solution.py:434
  39.0 7.5 %collective-permute-start.8 = (f32[3,16,128]{2,1,0:T(8,128)S(1)}, f32[3,16,128]{2,1,0:T(8,128)S(1)}, u32[]{:S(2)}, u32[]{:S(2)}) collective-permute-start(f32[3,16,128]{2,1,0:T(8,128)S(1)} %get-tuple-element.38), channel_id=1, source_target_pairs={{0,32},{16,48},{32,64},{48,80},{64,96},{80,112},{96,0},{112,16},{1... | collective-permute-start | bytes 73736 | tf_op jit(solution)/shard_map/ppermute | solution.py:439
  41.9 6.0 %collective-permute-start.9 = (f32[3,16,128]{2,1,0:T(8,128)S(1)}, f32[3,16,128]{2,1,0:T(8,128)S(1)}, u32[]{:S(2)}, u32[]{:S(2)}) collective-permute-start(f32[3,16,128]{2,1,0:T(8,128)S(1)} %get-tuple-element.39), channel_id=1, source_target_pairs={{0,64},{16,80},{32,96},{48,112},{64,0},{80,16},{96,32},{112,48},{1... | collective-permute-start | bytes 73736 | tf_op jit(solution)/shard_map/ppermute | solution.py:439
  45.8 3.8 %collective-permute-start.10 = (f32[3,16,128]{2,1,0:T(8,128)S(1)}, f32[3,16,128]{2,1,0:T(8,128)S(1)}, u32[]{:S(2)}, u32[]{:S(2)}) collective-permute-start(f32[3,16,128]{2,1,0:T(8,128)S(1)} %get-tuple-element.40), channel_id=1, source_target_pairs={{0,96},{16,112},{32,0},{48,16},{64,32},{80,48},{96,64},{112,80},{1... | collective-permute-start | bytes 73736 | tf_op jit(solution)/shard_map/ppermute | solution.py:439
  50.5 16.3 %all-to-all-start.2 = ((f32[16,3,16,128]{3,2,1,0:T(8,128)}), f32[16,3,16,128]{3,2,1,0:T(8,128)S(1)}, u32[]{:S(2)}, u32[]{:S(2)}) async-start(f32[16,3,16,128]{3,2,1,0:T(8,128)} %get-tuple-element.43), calls=%async_computation.2 | async-start | bytes 786432 | tf_op jit(solution)/shard_map/all_to_all | solution.py:443
  57.4 3.9 %collective-permute-start.16 = (f32[3,16,128]{2,1,0:T(8,128)S(1)}, f32[3,16,128]{2,1,0:T(8,128)S(1)}, u32[]{:S(2)}, u32[]{:S(2)}) collective-permute-start(f32[3,16,128]{2,1,0:T(8,128)S(1)} %get-tuple-element.44), channel_id=1, source_target_pairs={{0,96},{16,112},{32,0},{48,16},{64,32},{80,48},{96,64},{112,80},{1... | collective-permute-start | bytes 73736 | tf_op jit(solution)/shard_map/ppermute | solution.py:439
  59.6 5.3 %collective-permute-start.14 = (f32[3,16,128]{2,1,0:T(8,128)S(1)}, f32[3,16,128]{2,1,0:T(8,128)S(1)}, u32[]{:S(2)}, u32[]{:S(2)}) collective-permute-start(f32[3,16,128]{2,1,0:T(8,128)S(1)} %get-tuple-element.44), channel_id=1, source_target_pairs={{0,64},{16,80},{32,96},{48,112},{64,0},{80,16},{96,32},{112,48},{1... | collective-permute-start | bytes 73736 | tf_op jit(solution)/shard_map/ppermute | solution.py:439
  59.6 5.3 %collective-permute-start.12 = (f32[3,16,128]{2,1,0:T(8,128)S(1)}, f32[3,16,128]{2,1,0:T(8,128)S(1)}, u32[]{:S(2)}, u32[]{:S(2)}) collective-permute-start(f32[3,16,128]{2,1,0:T(8,128)S(1)} %get-tuple-element.44), channel_id=1, source_target_pairs={{0,32},{16,48},{32,64},{48,80},{64,96},{80,112},{96,0},{112,16},{1... | collective-permute-start | bytes 73736 | tf_op jit(solution)/shard_map/ppermute | solution.py:439
  60.5 4.9 %collective-permute-start.11 = (f32[3,16,128]{2,1,0:T(8,128)S(1)}, f32[3,16,128]{2,1,0:T(8,128)S(1)}, u32[]{:S(2)}, u32[]{:S(2)}) collective-permute-start(f32[3,16,128]{2,1,0:T(8,128)S(1)} %get-tuple-element.44), channel_id=1, source_target_pairs={{0,16},{16,0},{32,48},{48,32},{64,80},{80,64},{96,112},{112,96},{1... | collective-permute-start | bytes 73736 | tf_op jit(solution)/shard_map/ppermute | solution.py:434
  61.3 4.1 %collective-permute-start.17 = (f32[3,16,128]{2,1,0:T(8,128)S(1)}, f32[3,16,128]{2,1,0:T(8,128)S(1)}, u32[]{:S(2)}, u32[]{:S(2)}) collective-permute-start(f32[3,16,128]{2,1,0:T(8,128)S(1)} %collective-permute-done.16.refs_9_), channel_id=1, source_target_pairs={{0,16},{16,0},{32,48},{48,32},{64,80},{80,64},{96,112},{112,96},{1... | collective-permute-start | bytes 73736 | tf_op jit(solution)/shard_map/ppermute | solution.py:434
  64.9 1.2 %collective-permute-start.15 = (f32[3,16,128]{2,1,0:T(8,128)S(1)}, f32[3,16,128]{2,1,0:T(8,128)S(1)}, u32[]{:S(2)}, u32[]{:S(2)}) collective-permute-start(f32[3,16,128]{2,1,0:T(8,128)S(1)} %collective-permute-done.14.refs_7_), channel_id=1, source_target_pairs={{0,16},{16,0},{32,48},{48,32},{64,80},{80,64},{96,112},{112,96},{1... | collective-permute-start | bytes 73736 | tf_op jit(solution)/shard_map/ppermute | solution.py:434
  64.9 1.4 %collective-permute-start.13 = (f32[3,16,128]{2,1,0:T(8,128)S(1)}, f32[3,16,128]{2,1,0:T(8,128)S(1)}, u32[]{:S(2)}, u32[]{:S(2)}) collective-permute-start(f32[3,16,128]{2,1,0:T(8,128)S(1)} %collective-permute-done.12.refs_5_), channel_id=1, source_target_pairs={{0,16},{16,0},{32,48},{48,32},{64,80},{80,64},{96,112},{112,96},{1... | collective-permute-start | bytes 73736 | tf_op jit(solution)/shard_map/ppermute | solution.py:434
  71.2 19.2 %all-to-all-start.3 = ((f32[16,3,16,128]{3,2,1,0:T(8,128)}), f32[16,3,16,128]{3,2,1,0:T(8,128)S(1)}, u32[]{:S(2)}, u32[]{:S(2)}) async-start(f32[16,3,16,128]{3,2,1,0:T(8,128)} %bitcast.4), calls=%async_computation.3 | async-start | bytes 786432 | tf_op jit(solution)/shard_map/all_to_all | solution.py:443
  79.4 1.4 %collective-permute-start.18 = (f32[4,3,16,128]{3,2,1,0:T(8,128)S(1)}, f32[4,3,16,128]{3,2,1,0:T(8,128)S(1)}, u32[]{:S(2)}, u32[]{:S(2)}) collective-permute-start(f32[4,3,16,128]{3,2,1,0:T(8,128)S(1)} %get-tuple-element.47), channel_id=1, source_target_pairs={{0,16},{16,0},{32,48},{48,32},{64,80},{80,64},{96,112},{112,96},{1... | collective-permute-start | bytes 294920 | tf_op jit(solution)/shard_map/ppermute | solution.py:434
  80.9 5.2 %collective-permute-start.19 = (f32[3,16,128]{2,1,0:T(8,128)S(1)}, f32[3,16,128]{2,1,0:T(8,128)S(1)}, u32[]{:S(2)}, u32[]{:S(2)}) collective-permute-start(f32[3,16,128]{2,1,0:T(8,128)S(1)} %get-tuple-element.49), channel_id=1, source_target_pairs={{0,32},{16,48},{32,64},{48,80},{64,96},{80,112},{96,0},{112,16},{1... | collective-permute-start | bytes 73736 | tf_op jit(solution)/shard_map/ppermute | solution.py:439
  80.9 5.4 %collective-permute-start.20 = (f32[3,16,128]{2,1,0:T(8,128)S(1)}, f32[3,16,128]{2,1,0:T(8,128)S(1)}, u32[]{:S(2)}, u32[]{:S(2)}) collective-permute-start(f32[3,16,128]{2,1,0:T(8,128)S(1)} %get-tuple-element.50), channel_id=1, source_target_pairs={{0,64},{16,80},{32,96},{48,112},{64,0},{80,16},{96,32},{112,48},{1... | collective-permute-start | bytes 73736 | tf_op jit(solution)/shard_map/ppermute | solution.py:439
  84.1 3.8 %collective-permute-start.21 = (f32[3,16,128]{2,1,0:T(8,128)S(1)}, f32[3,16,128]{2,1,0:T(8,128)S(1)}, u32[]{:S(2)}, u32[]{:S(2)}) collective-permute-start(f32[3,16,128]{2,1,0:T(8,128)S(1)} %get-tuple-element.51), channel_id=1, source_target_pairs={{0,96},{16,112},{32,0},{48,16},{64,32},{80,48},{96,64},{112,80},{1... | collective-permute-start | bytes 73736 | tf_op jit(solution)/shard_map/ppermute | solution.py:439

commit v2 on v1

--- a/solution.py
+++ b/solution.py
@@ -117,9 +117,9 @@
         col_refs = refs[4:3 + n_row]
         rowf_ref, mine_ref, sibling_ref = refs[3 + n_row:6 + n_row]
         refs = refs[6 + n_row:]
-    list_ref, pat_ref, rows_ref, cols_ref, colf_ref, stiff_ref, d_ref, z_ref, sems, list_sem, state_sems = refs[:11]
+    list_ref, pat_ref, rows_ref, cols_ref, colf_ref, rowsum_ref, stiff_ref, d_ref, z_ref, sems, list_sem, state_sems = refs[:12]
     if fresh:
-        bonds_ref, cracks_ref, out_sems = refs[11:]
+        bonds_ref, cracks_ref, out_sems = refs[12:]
     n_col, n_z = row_ref.shape[0], n_row // CORES
     full = 8 * TILE_DEV
     part = 3 * TILE_DEV
@@ -147,15 +147,17 @@
         return carry
 
     begin(0, 0)
+    used_rows = rows_ref.at[pl.ds(0, n_col * full)]
+    used_cols = cols_ref.at[pl.ds(0, n_row * full)]
     if fresh:
         states = (
-            pltpu.make_async_copy(rows_ref, all_rows_ref, state_sems.at[0]),
-            pltpu.make_async_copy(cols_ref, all_cols_ref, state_sems.at[1]),
+            pltpu.make_async_copy(used_rows, all_rows_ref, state_sems.at[0]),
+            pltpu.make_async_copy(used_cols, all_cols_ref, state_sems.at[1]),
         )
     else:
         states = (
-            pltpu.make_async_copy(all_rows_ref, rows_ref, state_sems.at[0]),
-            pltpu.make_async_copy(all_cols_ref, cols_ref, state_sems.at[1]),
+            pltpu.make_async_copy(all_rows_ref, used_rows, state_sems.at[0]),
+            pltpu.make_async_copy(all_cols_ref, used_cols, state_sems.at[1]),
         )
         for copy in states:
             copy.start()
@@ -166,7 +168,7 @@
     chunks = (live + UNROLL - 1) // UNROLL
 
     lax.fori_loop(1, chunks, begin, 0)
-    rowf_ref[...] = jnp.zeros_like(rowf_ref)
+    rowsum_ref[...] = jnp.zeros_like(rowsum_ref)
     colf_ref[...] = jnp.zeros_like(colf_ref)
     if not fresh:
         for copy in states:
@@ -215,7 +217,7 @@
             d = ahead.pop(j - LEAD)
             inv_now, inv_rest = inverse_lengths(d)
             on_owner = sum_owner(other[1], weights(inv_now, inv_rest, stiffness(d, inv_rest)))
-            add(rowf_ref, t, post(on_owner, state, mine[2]))
+            add(rowsum_ref, t, post(on_owner, state, mine[2]))
 
     def pair(slot):
         return list_ref[0, slot].astype(jnp.int32), list_ref[1, slot].astype(jnp.int32)
@@ -264,13 +266,14 @@
             so, sp = tiles(first + j)
             alive = jnp.where(first + j < live, 1.0, 0.0)
             o, p = pair(first + j)
-            add(rowf_ref, o, post(on_owner, so, row_of(so, 3) * alive))
+            add(rowsum_ref, o, post(on_owner, so, row_of(so, 3) * alive))
             add(colf_ref, p, post(on_partner, sp, row_of(sp, 3) * alive))
         if fresh:
             store(i).start()
         return carry
 
     lax.fori_loop(0, chunks, body, 0)
+    rowf_ref[...] = rowsum_ref[:n_col * part]
     for i in range(n_z):
         for ref, c in ((mine_ref, core), (sibling_ref, 1 - core)):
             start = pl.multiple_of((i * CORES + c) * part, part)
@@ -302,9 +305,10 @@
         scratch_shapes=[
             pltpu.SMEM(ids.shape, ids.dtype),
             pltpu.VMEM((3, 64, TILE), jnp.bfloat16),
-            pltpu.VMEM(held[0].shape, jnp.float32),
-            pltpu.VMEM(held[1].shape, jnp.float32),
-            pltpu.VMEM((n_row * 3 * TILE_DEV, TILE), jnp.float32),
+            pltpu.VMEM((held[0].shape[0] + 8 * TILE_DEV, TILE), jnp.float32),
+            pltpu.VMEM((held[1].shape[0] + 8 * TILE_DEV, TILE), jnp.float32),
+            pltpu.VMEM(((n_row + 1) * 3 * TILE_DEV, TILE), jnp.float32),
+            pltpu.VMEM(((n_col + 1) * 3 * TILE_DEV, TILE), jnp.float32),
             pltpu.VMEM(held[2].shape, jnp.float32),
             pltpu.VMEM((LEAD, TILE, (3 if fresh else 2) * TILE), jnp.float32),
             pltpu.VMEM((LEAD, 2, 16, TILE), jnp.bfloat16),

time: 92.3 us -> 93 us (level)
  Pallas kernels: 13.7 us -> 15.7 us
  starting transfers between devices: 49.1 us -> 47.4 us
    all_to_all x4, starting transfers between devices: 26.9 us -> 23.4 us  [swap(): return lax.all_to_all(x, 'col', 0, 0, tiled=True)]
    pallas_call x2, Pallas kernels: 10.2 us -> 12.1 us  [pair_forces(): pl.pallas_call(functools.partial(pair_kernel, n_row, fresh), out_shape=ou...]
    ppermute x12, waiting for transfers between devices: 14.7 us -> 16.5 us  [along_z(): lax.ppermute(x, 'row', [(i, (i // CORES + d) % n_z * CORES + i % CORES) f...]
    all_to_all x4, waiting for transfers between devices: 7.42 us -> 5.81 us  [swap(): return lax.all_to_all(x, 'col', 0, 0, tiled=True)]
    ppermute x12, starting transfers between devices: 20.9 us -> 22.3 us  [along_z(): lax.ppermute(x, 'row', [(i, (i // CORES + d) % n_z * CORES + i % CORES) f...]
  transfers between devices with their start and end apart: 26 -> 26, of which waited for: 19 -> 20; matrix products, arithmetic and copies ran while one was open for 0% -> 0% of each run, Pallas kernels for 0% -> 0%
where the time goes in v2:
time: 93 us; the launch traced here: 91.4 us
  starting transfers between devices  47.4 us (51%)
  waiting for transfers between devices  26.3 us (28%)
  Pallas kernels  15.7 us (17%)
  between operations  1.37 us (1%)
    all_to_all x4, starting transfers between devices, swap(): return lax.all_to_all(x, 'col', 0, 0, tiled=True)  23.4 us
    ppermute x12, starting transfers between devices, along_z(): lax.ppermute(x, 'row', [(i, (i // CORES + d) % n_z * CORES + i % CORES) f...  22.3 us
    ppermute x12, waiting for transfers between devices, along_z(): lax.ppermute(x, 'row', [(i, (i // CORES + d) % n_z * CORES + i % CORES) f...  16.5 us
    pallas_call x2, Pallas kernels, pair_forces(): pl.pallas_call(functools.partial(pair_kernel, n_row, fresh), out_shape=ou...  12.1 us
    all_to_all x4, waiting for transfers between devices, swap(): return lax.all_to_all(x, 'col', 0, 0, tiled=True)  5.81 us
    ppermute x10, waiting for transfers between devices, to_sibling(): return lax.ppermute(x, 'row', [(i, i ^ 1) for i in range(n_row)])  4.01 us
    pallas_call x1, Pallas kernels, start(): pl.pallas_call(start_kernel, out_shape=(f32(n_col, 7, TILE_DEV, TILE), f3...  1.96 us
  transfers between devices with their start and end apart: 26, of which 20 were waited for; matrix products, arithmetic and copies ran while one was open for 0% of the time, Pallas kernels for 0%

profile of v2, /device:TPU:0, one launch (start us, length us, event | category | flops | bytes accessed | tf_op | source)
XLA Modules:
  0.0 91.4 jit_solution(13520568441338776974)
XLA Ops:
  1.3 2.0 %first_half_step.1 = (f32[16,7,16,128]{3,2,1,0:T(8,128)}, f32[7,16,128]{2,1,0:T(8,128)}, f32[3,16,128]{2,1,0:T(8,128)}, f32[3,16,128]{2,1,0:T(8,128)}, f32[5,128]{1,0:T(8,128)}) custom-call(f32[2]{0:T(128)} %moduli_ref.1, s32[1]{0:T(128)S(6)} %copy.13.count_ref, s32[1,128]{1,0:T(1,128)} %bitcast.6, s32[1,128]{1,0:T(1,128)} %bitcast.7, s32[16,128]{1,0:T(8,128)} %bitcast.5, ...), custom_call_target="tpu_custom_call" | custom-call | tf_op jit(solution)/shard_map/first_half_step/pallas_call | solution.py:350
  3.2 7.1 %all-to-all-start = ((f32[16,7,16,128]{3,2,1,0:T(8,128)}), f32[16,7,16,128]{3,2,1,0:T(8,128)S(1)}, u32[]{:S(2)}, u32[]{:S(2)}) async-start(f32[16,7,16,128]{3,2,1,0:T(8,128)} %get-tuple-element.29), calls=%async_computation | async-start | bytes 1835008 | tf_op jit(solution)/shard_map/all_to_all | solution.py:447
  10.4 4.1 %collective-permute-start.5 = (f32[7,16,128]{2,1,0:T(8,128)}, f32[7,16,128]{2,1,0:T(8,128)S(1)}, u32[]{:S(2)}, u32[]{:S(2)}) collective-permute-start(f32[7,16,128]{2,1,0:T(8,128)} %get-tuple-element.30.refs_4_), channel_id=1, source_target_pairs={{0,96},{16,112},{32,0},{48,16},{64,32},{80,48},{96,64},{112,80},{1... | collective-permute-start | bytes 172040 | tf_op jit(solution)/shard_map/ppermute | solution.py:443
  14.5 0.0 collective-permute-start.3
  14.5 1.3 %collective-permute-start.1 = (f32[7,16,128]{2,1,0:T(8,128)}, f32[7,16,128]{2,1,0:T(8,128)S(1)}, u32[]{:S(2)}, u32[]{:S(2)}) collective-permute-start(f32[7,16,128]{2,1,0:T(8,128)} %get-tuple-element.30.refs_4_), channel_id=1, source_target_pairs={{0,32},{16,48},{32,64},{48,80},{64,96},{80,112},{96,0},{112,16},{1... | collective-permute-start | bytes 172040 | tf_op jit(solution)/shard_map/ppermute | solution.py:443
  15.7 0.0 collective-permute-start
  15.7 0.9 collective-permute-done.5.refs_8_
  16.6 3.8 %collective-permute-done.3.refs_6_ = f32[7,16,128]{2,1,0:T(8,128)S(1)} collective-permute-done((f32[7,16,128]{2,1,0:T(8,128)}, f32[7,16,128]{2,1,0:T(8,128)S(1)}, u32[]{:S(2)}, u32[]{:S(2)}) %collective-permute-start.3) | collective-permute-done | bytes 57376 | tf_op jit(solution)/shard_map/ppermute | solution.py:443
  20.4 0.0 collective-permute-start.4
  20.4 0.3 collective-permute-done.1.refs_4_
  20.7 0.2 collective-permute-start.2
  20.9 0.0 collective-permute-done.refs_3_
  20.9 0.0 collective-permute-done.6.refs_9_
  20.9 0.7 collective-permute-done.4.refs_7_
  21.7 0.3 collective-permute-done.2.refs_5_
  21.9 4.5 %all-to-all-done.refs_2_ = f32[16,7,16,128]{3,2,1,0:T(8,128)S(1)} async-done(((f32[16,7,16,128]{3,2,1,0:T(8,128)}), f32[16,7,16,128]{3,2,1,0:T(8,128)S(1)}, u32[]{:S(2)}, u32[]{:S(2)}) %all-to-all-start) | async-done | bytes 917536 | tf_op jit(solution)/shard_map/all_to_all | solution.py:447
  26.4 0.7 copy-done.3
  27.1 6.8 %pair_forces.1 = (f32[768,128]{1,0:T(8,128)}, f32[4,3,16,128]{3,2,1,0:T(8,128)S(1)}, f32[4,3,16,128]{3,2,1,0:T(8,128)S(1)}, f32[2048,128]{1,0:T(8,128)S(1)}, f32...) custom-call(f32[5,128]{1,0:T(8,128)S(1)} %copy-done.3, s32[128,128,128]{2,1,0:T(8,128)} %refs_0_.1, ...), custom_call_target="tpu_custom_call" | custom-call | tf_op jit(solution)/shard_map/pair_forces/pallas_call | solution.py:300
  33.9 3.6 %all-to-all-start.1 = ((f32[16,3,16,128]{3,2,1,0:T(8,128)}), f32[16,3,16,128]{3,2,1,0:T(8,128)S(1)}, u32[]{:S(2)}, u32[]{:S(2)}) async-start(f32[16,3,16,128]{3,2,1,0:T(8,128)} %bitcast.3), calls=%async_computation.1 | async-start | bytes 786432 | tf_op jit(solution)/shard_map/all_to_all | solution.py:447
  37.5 0.3 collective-permute-start.7
  37.7 1.1 %collective-permute-done.7.other_ref = f32[4,3,16,128]{3,2,1,0:T(8,128)S(1)} collective-permute-done((f32[4,3,16,128]{3,2,1,0:T(8,128)S(1)}, f32[4,3,16,128]{3,2,1,0:T(8,128)S(1)}, u32[]{:S(2)}, u32[]{:S(2)}) %collective-permute-start.7) | collective-permute-done | bytes 98336 | tf_op jit(solution)/shard_map/ppermute | solution.py:438
  38.9 2.2 %collective-permute-start.8 = (f32[3,16,128]{2,1,0:T(8,128)S(1)}, f32[3,16,128]{2,1,0:T(8,128)S(1)}, u32[]{:S(2)}, u32[]{:S(2)}) collective-permute-start(f32[3,16,128]{2,1,0:T(8,128)S(1)} %get-tuple-element.38), channel_id=1, source_target_pairs={{0,32},{16,48},{32,64},{48,80},{64,96},{80,112},{96,0},{112,16},{1... | collective-permute-start | bytes 73736 | tf_op jit(solution)/shard_map/ppermute | solution.py:443
  41.0 5.4 %collective-permute-start.9 = (f32[3,16,128]{2,1,0:T(8,128)S(1)}, f32[3,16,128]{2,1,0:T(8,128)S(1)}, u32[]{:S(2)}, u32[]{:S(2)}) collective-permute-start(f32[3,16,128]{2,1,0:T(8,128)S(1)} %get-tuple-element.39), channel_id=1, source_target_pairs={{0,64},{16,80},{32,96},{48,112},{64,0},{80,16},{96,32},{112,48},{1... | collective-permute-start | bytes 73736 | tf_op jit(solution)/shard_map/ppermute | solution.py:443
  46.4 0.3 collective-permute-done.8.refs_1_
  46.7 1.7 %collective-permute-done.9.refs_2_ = f32[3,16,128]{2,1,0:T(8,128)S(1)} collective-permute-done((f32[3,16,128]{2,1,0:T(8,128)S(1)}, f32[3,16,128]{2,1,0:T(8,128)S(1)}, u32[]{:S(2)}, u32[]{:S(2)}) %collective-permute-start.9) | collective-permute-done | bytes 24608 | tf_op jit(solution)/shard_map/ppermute | solution.py:443
  48.5 1.8 %collective-permute-done.10.refs_3_ = f32[3,16,128]{2,1,0:T(8,128)S(1)} collective-permute-done((f32[3,16,128]{2,1,0:T(8,128)S(1)}, f32[3,16,128]{2,1,0:T(8,128)S(1)}, u32[]{:S(2)}, u32[]{:S(2)}) %collective-permute-start.10) | collective-permute-done | bytes 24608 | tf_op jit(solution)/shard_map/ppermute | solution.py:443
  50.2 0.9 next_step.1
  51.1 6.9 %all-to-all-start.2 = ((f32[16,3,16,128]{3,2,1,0:T(8,128)}), f32[16,3,16,128]{3,2,1,0:T(8,128)S(1)}, u32[]{:S(2)}, u32[]{:S(2)}) async-start(f32[16,3,16,128]{3,2,1,0:T(8,128)} %get-tuple-element.43), calls=%async_computation.2 | async-start | bytes 786432 | tf_op jit(solution)/shard_map/all_to_all | solution.py:447
  58.0 1.3 %collective-permute-start.16 = (f32[3,16,128]{2,1,0:T(8,128)S(1)}, f32[3,16,128]{2,1,0:T(8,128)S(1)}, u32[]{:S(2)}, u32[]{:S(2)}) collective-permute-start(f32[3,16,128]{2,1,0:T(8,128)S(1)} %get-tuple-element.44), channel_id=1, source_target_pairs={{0,96},{16,112},{32,0},{48,16},{64,32},{80,48},{96,64},{112,80},{1... | collective-permute-start | bytes 73736 | tf_op jit(solution)/shard_map/ppermute | solution.py:443
  59.2 0.6 collective-permute-start.14
  59.8 1.2 %collective-permute-start.12 = (f32[3,16,128]{2,1,0:T(8,128)S(1)}, f32[3,16,128]{2,1,0:T(8,128)S(1)}, u32[]{:S(2)}, u32[]{:S(2)}) collective-permute-start(f32[3,16,128]{2,1,0:T(8,128)S(1)} %get-tuple-element.44), channel_id=1, source_target_pairs={{0,32},{16,48},{32,64},{48,80},{64,96},{80,112},{96,0},{112,16},{1... | collective-permute-start | bytes 73736 | tf_op jit(solution)/shard_map/ppermute | solution.py:443
  61.0 0.9 collective-permute-done.16.refs_9_
  61.9 2.7 %collective-permute-done.14.refs_7_ = f32[3,16,128]{2,1,0:T(8,128)S(1)} collective-permute-done((f32[3,16,128]{2,1,0:T(8,128)S(1)}, f32[3,16,128]{2,1,0:T(8,128)S(1)}, u32[]{:S(2)}, u32[]{:S(2)}) %collective-permute-start.14) | collective-permute-done | bytes 24608 | tf_op jit(solution)/shard_map/ppermute | solution.py:443
  64.6 0.3 collective-permute-done.12.refs_5_
  64.9 0.2 collective-permute-start.13
  65.1 0.7 collective-permute-done.15.refs_8_
  65.8 0.3 collective-permute-done.13.refs_6_
  66.0 1.3 %all-to-all-done.2.refs_3_ = f32[16,3,16,128]{3,2,1,0:T(8,128)S(1)} async-done(((f32[16,3,16,128]{3,2,1,0:T(8,128)}), f32[16,3,16,128]{3,2,1,0:T(8,128)S(1)}, u32[]{:S(2)}, u32[]{:S(2)}) %all-to-all-start.2) | async-done | bytes 393248 | tf_op jit(solution)/shard_map/all_to_all | solution.py:447
  67.4 5.4 %pair_forces_again.1 = (f32[768,128]{1,0:T(8,128)}, f32[4,3,16,128]{3,2,1,0:T(8,128)S(1)}, f32[4,3,16,128]{3,2,1,0:T(8,128)S(1)}) custom-call(f32[5,128]{1,0:T(8,128)S(1)} %copy-done.4, f32[2048,128]{1,0:T(8,128)S(1)} %get-tuple-element.31.refs_0_, f32[1024,128]{1,0:T(8,128)S(1)} %get-tuple-element.32.refs_1_, f32[128,128,128]{2,1,0:T(8,128)} %get-tuple-element.33.refs_2_, ...), custom_call_target="tpu_custom_call" | custom-call | tf_op jit(solution)/shard_map/pair_forces_again/pallas_call | solution.py:300
  72.7 5.9 %all-to-all-start.3 = ((f32[16,3,16,128]{3,2,1,0:T(8,128)}), f32[16,3,16,128]{3,2,1,0:T(8,128)S(1)}, u32[]{:S(2)}, u32[]{:S(2)}) async-start(f32[16,3,16,128]{3,2,1,0:T(8,128)} %bitcast.4), calls=%async_computation.3 | async-start | bytes 786432 | tf_op jit(solution)/shard_map/all_to_all | solution.py:447
  78.6 1.0 %collective-permute-start.18 = (f32[4,3,16,128]{3,2,1,0:T(8,128)S(1)}, f32[4,3,16,128]{3,2,1,0:T(8,128)S(1)}, u32[]{:S(2)}, u32[]{:S(2)}) collective-permute-start(f32[4,3,16,128]{3,2,1,0:T(8,128)S(1)} %get-tuple-element.47), channel_id=1, source_target_pairs={{0,16},{16,0},{32,48},{48,32},{64,80},{80,64},{96,112},{112,96},{1... | collective-permute-start | bytes 294920 | tf_op jit(solution)/shard_map/ppermute | solution.py:438
  79.6 0.9 %collective-permute-done.18.other_ref = f32[4,3,16,128]{3,2,1,0:T(8,128)S(1)} collective-permute-done((f32[4,3,16,128]{3,2,1,0:T(8,128)S(1)}, f32[4,3,16,128]{3,2,1,0:T(8,128)S(1)}, u32[]{:S(2)}, u32[]{:S(2)}) %collective-permute-start.18) | collective-permute-done | bytes 98336 | tf_op jit(solution)/shard_map/ppermute | solution.py:438
  80.6 1.2 %collective-permute-start.19 = (f32[3,16,128]{2,1,0:T(8,128)S(1)}, f32[3,16,128]{2,1,0:T(8,128)S(1)}, u32[]{:S(2)}, u32[]{:S(2)}) collective-permute-start(f32[3,16,128]{2,1,0:T(8,128)S(1)} %get-tuple-element.49), channel_id=1, source_target_pairs={{0,32},{16,48},{32,64},{48,80},{64,96},{80,112},{96,0},{112,16},{1... | collective-permute-start | bytes 73736 | tf_op jit(solution)/shard_map/ppermute | solution.py:443
  81.7 5.2 %collective-permute-start.20 = (f32[3,16,128]{2,1,0:T(8,128)S(1)}, f32[3,16,128]{2,1,0:T(8,128)S(1)}, u32[]{:S(2)}, u32[]{:S(2)}) collective-permute-start(f32[3,16,128]{2,1,0:T(8,128)S(1)} %get-tuple-element.50), channel_id=1, source_target_pairs={{0,64},{16,80},{32,96},{48,112},{64,0},{80,16},{96,32},{112,48},{1... | collective-permute-start | bytes 73736 | tf_op jit(solution)/shard_map/ppermute | solution.py:443
  86.9 0.3 collective-permute-done.19.refs_1_
  87.2 1.7 %collective-permute-done.20.refs_2_ = f32[3,16,128]{2,1,0:T(8,128)S(1)} collective-permute-done((f32[3,16,128]{2,1,0:T(8,128)S(1)}, f32[3,16,128]{2,1,0:T(8,128)S(1)}, u32[]{:S(2)}, u32[]{:S(2)}) %collective-permute-start.20) | collective-permute-done | bytes 24608 | tf_op jit(solution)/shard_map/ppermute | solution.py:443
  89.0 1.8 %collective-permute-done.21.refs_3_ = f32[3,16,128]{2,1,0:T(8,128)S(1)} collective-permute-done((f32[3,16,128]{2,1,0:T(8,128)S(1)}, f32[3,16,128]{2,1,0:T(8,128)S(1)}, u32[]{:S(2)}, u32[]{:S(2)}) %collective-permute-start.21) | collective-permute-done | bytes 24608 | tf_op jit(solution)/shard_map/ppermute | solution.py:443
  90.7 0.7 last_half_step.1
  (21 shorter events, 0.1 us)
Async XLA Ops:
  3.2 23.2 %all-to-all-start = ((f32[16,7,16,128]{3,2,1,0:T(8,128)}), f32[16,7,16,128]{3,2,1,0:T(8,128)S(1)}, u32[]{:S(2)}, u32[]{:S(2)}) async-start(f32[16,7,16,128]{3,2,1,0:T(8,128)} %get-tuple-element.29), calls=%async_computation | async-start | bytes 1835008 | tf_op jit(solution)/shard_map/all_to_all | solution.py:447
  10.4 6.3 %collective-permute-start.5 = (f32[7,16,128]{2,1,0:T(8,128)}, f32[7,16,128]{2,1,0:T(8,128)S(1)}, u32[]{:S(2)}, u32[]{:S(2)}) collective-permute-start(f32[7,16,128]{2,1,0:T(8,128)} %get-tuple-element.30.refs_4_), channel_id=1, source_target_pairs={{0,96},{16,112},{32,0},{48,16},{64,32},{80,48},{96,64},{112,80},{1... | collective-permute-start | bytes 172040 | tf_op jit(solution)/shard_map/ppermute | solution.py:443
  14.5 5.9 %collective-permute-start.3 = (f32[7,16,128]{2,1,0:T(8,128)}, f32[7,16,128]{2,1,0:T(8,128)S(1)}, u32[]{:S(2)}, u32[]{:S(2)}) collective-permute-start(f32[7,16,128]{2,1,0:T(8,128)} %get-tuple-element.30.refs_4_), channel_id=1, source_target_pairs={{0,64},{16,80},{32,96},{48,112},{64,0},{80,16},{96,32},{112,48},{1... | collective-permute-start | bytes 172040 | tf_op jit(solution)/shard_map/ppermute | solution.py:443
  14.5 6.2 %collective-permute-start.1 = (f32[7,16,128]{2,1,0:T(8,128)}, f32[7,16,128]{2,1,0:T(8,128)S(1)}, u32[]{:S(2)}, u32[]{:S(2)}) collective-permute-start(f32[7,16,128]{2,1,0:T(8,128)} %get-tuple-element.30.refs_4_), channel_id=1, source_target_pairs={{0,32},{16,48},{32,64},{48,80},{64,96},{80,112},{96,0},{112,16},{1... | collective-permute-start | bytes 172040 | tf_op jit(solution)/shard_map/ppermute | solution.py:443
  15.7 5.2 %collective-permute-start = (f32[7,16,128]{2,1,0:T(8,128)}, f32[7,16,128]{2,1,0:T(8,128)S(1)}, u32[]{:S(2)}, u32[]{:S(2)}) collective-permute-start(f32[7,16,128]{2,1,0:T(8,128)} %get-tuple-element.30.refs_4_), channel_id=1, source_target_pairs={{0,16},{16,0},{32,48},{48,32},{64,80},{80,64},{96,112},{112,96},{1... | collective-permute-start | bytes 172040 | tf_op jit(solution)/shard_map/ppermute | solution.py:438
  16.6 4.3 %collective-permute-start.6 = (f32[7,16,128]{2,1,0:T(8,128)S(1)}, f32[7,16,128]{2,1,0:T(8,128)S(1)}, u32[]{:S(2)}, u32[]{:S(2)}) collective-permute-start(f32[7,16,128]{2,1,0:T(8,128)S(1)} %collective-permute-done.5.refs_8_), channel_id=1, source_target_pairs={{0,16},{16,0},{32,48},{48,32},{64,80},{80,64},{96,112},{112,96},{1... | collective-permute-start | bytes 172040 | tf_op jit(solution)/shard_map/ppermute | solution.py:438
  20.4 1.2 %collective-permute-start.4 = (f32[7,16,128]{2,1,0:T(8,128)S(1)}, f32[7,16,128]{2,1,0:T(8,128)S(1)}, u32[]{:S(2)}, u32[]{:S(2)}) collective-permute-start(f32[7,16,128]{2,1,0:T(8,128)S(1)} %collective-permute-done.3.refs_6_), channel_id=1, source_target_pairs={{0,16},{16,0},{32,48},{48,32},{64,80},{80,64},{96,112},{112,96},{1... | collective-permute-start | bytes 172040 | tf_op jit(solution)/shard_map/ppermute | solution.py:438
  20.7 1.2 %collective-permute-start.2 = (f32[7,16,128]{2,1,0:T(8,128)S(1)}, f32[7,16,128]{2,1,0:T(8,128)S(1)}, u32[]{:S(2)}, u32[]{:S(2)}) collective-permute-start(f32[7,16,128]{2,1,0:T(8,128)S(1)} %collective-permute-done.1.refs_4_), channel_id=1, source_target_pairs={{0,16},{16,0},{32,48},{48,32},{64,80},{80,64},{96,112},{112,96},{1... | collective-permute-start | bytes 172040 | tf_op jit(solution)/shard_map/ppermute | solution.py:438
  26.4 0.7 copy-start.3
  27.1 23.1 %copy-start = (f32[7,16,128]{2,1,0:T(8,128)S(1)}, f32[7,16,128]{2,1,0:T(8,128)}, u32[]{:S(2)}) copy-start(f32[7,16,128]{2,1,0:T(8,128)} %get-tuple-element.30.refs_4_) | copy-start | bytes 172036
  27.1 23.1 %copy-start.1 = (f32[3,16,128]{2,1,0:T(8,128)S(1)}, f32[3,16,128]{2,1,0:T(8,128)}, u32[]{:S(2)}) copy-start(f32[3,16,128]{2,1,0:T(8,128)} %get-tuple-element.41.refs_5_) | copy-start | bytes 73732
  27.1 23.1 %copy-start.2 = (f32[3,16,128]{2,1,0:T(8,128)S(1)}, f32[3,16,128]{2,1,0:T(8,128)}, u32[]{:S(2)}) copy-start(f32[3,16,128]{2,1,0:T(8,128)} %get-tuple-element.42.refs_6_) | copy-start | bytes 73732
  27.1 40.3 %copy-start.4 = (f32[5,128]{1,0:T(8,128)S(1)}, f32[5,128]{1,0:T(8,128)}, u32[]{:S(2)}) copy-start(f32[5,128]{1,0:T(8,128)} %get-tuple-element.28.ids_ref) | copy-start | bytes 7684
  33.9 16.3 %all-to-all-start.1 = ((f32[16,3,16,128]{3,2,1,0:T(8,128)}), f32[16,3,16,128]{3,2,1,0:T(8,128)S(1)}, u32[]{:S(2)}, u32[]{:S(2)}) async-start(f32[16,3,16,128]{3,2,1,0:T(8,128)} %bitcast.3), calls=%async_computation.1 | async-start | bytes 786432 | tf_op jit(solution)/shard_map/all_to_all | solution.py:447
  37.5 1.4 %collective-permute-start.7 = (f32[4,3,16,128]{3,2,1,0:T(8,128)S(1)}, f32[4,3,16,128]{3,2,1,0:T(8,128)S(1)}, u32[]{:S(2)}, u32[]{:S(2)}) collective-permute-start(f32[4,3,16,128]{3,2,1,0:T(8,128)S(1)} %get-tuple-element.36), channel_id=1, source_target_pairs={{0,16},{16,0},{32,48},{48,32},{64,80},{80,64},{96,112},{112,96},{1... | collective-permute-start | bytes 294920 | tf_op jit(solution)/shard_map/ppermute | solution.py:438
  38.9 7.9 %collective-permute-start.8 = (f32[3,16,128]{2,1,0:T(8,128)S(1)}, f32[3,16,128]{2,1,0:T(8,128)S(1)}, u32[]{:S(2)}, u32[]{:S(2)}) collective-permute-start(f32[3,16,128]{2,1,0:T(8,128)S(1)} %get-tuple-element.38), channel_id=1, source_target_pairs={{0,32},{16,48},{32,64},{48,80},{64,96},{80,112},{96,0},{112,16},{1... | collective-permute-start | bytes 73736 | tf_op jit(solution)/shard_map/ppermute | solution.py:443
  41.0 7.4 %collective-permute-start.9 = (f32[3,16,128]{2,1,0:T(8,128)S(1)}, f32[3,16,128]{2,1,0:T(8,128)S(1)}, u32[]{:S(2)}, u32[]{:S(2)}) collective-permute-start(f32[3,16,128]{2,1,0:T(8,128)S(1)} %get-tuple-element.39), channel_id=1, source_target_pairs={{0,64},{16,80},{32,96},{48,112},{64,0},{80,16},{96,32},{112,48},{1... | collective-permute-start | bytes 73736 | tf_op jit(solution)/shard_map/ppermute | solution.py:443
  46.4 3.8 %collective-permute-start.10 = (f32[3,16,128]{2,1,0:T(8,128)S(1)}, f32[3,16,128]{2,1,0:T(8,128)S(1)}, u32[]{:S(2)}, u32[]{:S(2)}) collective-permute-start(f32[3,16,128]{2,1,0:T(8,128)S(1)} %get-tuple-element.40), channel_id=1, source_target_pairs={{0,96},{16,112},{32,0},{48,16},{64,32},{80,48},{96,64},{112,80},{1... | collective-permute-start | bytes 73736 | tf_op jit(solution)/shard_map/ppermute | solution.py:443
  51.1 16.3 %all-to-all-start.2 = ((f32[16,3,16,128]{3,2,1,0:T(8,128)}), f32[16,3,16,128]{3,2,1,0:T(8,128)S(1)}, u32[]{:S(2)}, u32[]{:S(2)}) async-start(f32[16,3,16,128]{3,2,1,0:T(8,128)} %get-tuple-element.43), calls=%async_computation.2 | async-start | bytes 786432 | tf_op jit(solution)/shard_map/all_to_all | solution.py:447
  58.0 3.9 %collective-permute-start.16 = (f32[3,16,128]{2,1,0:T(8,128)S(1)}, f32[3,16,128]{2,1,0:T(8,128)S(1)}, u32[]{:S(2)}, u32[]{:S(2)}) collective-permute-start(f32[3,16,128]{2,1,0:T(8,128)S(1)} %get-tuple-element.44), channel_id=1, source_target_pairs={{0,96},{16,112},{32,0},{48,16},{64,32},{80,48},{96,64},{112,80},{1... | collective-permute-start | bytes 73736 | tf_op jit(solution)/shard_map/ppermute | solution.py:443
  59.2 5.3 %collective-permute-start.14 = (f32[3,16,128]{2,1,0:T(8,128)S(1)}, f32[3,16,128]{2,1,0:T(8,128)S(1)}, u32[]{:S(2)}, u32[]{:S(2)}) collective-permute-start(f32[3,16,128]{2,1,0:T(8,128)S(1)} %get-tuple-element.44), channel_id=1, source_target_pairs={{0,64},{16,80},{32,96},{48,112},{64,0},{80,16},{96,32},{112,48},{1... | collective-permute-start | bytes 73736 | tf_op jit(solution)/shard_map/ppermute | solution.py:443
  59.8 5.0 %collective-permute-start.12 = (f32[3,16,128]{2,1,0:T(8,128)S(1)}, f32[3,16,128]{2,1,0:T(8,128)S(1)}, u32[]{:S(2)}, u32[]{:S(2)}) collective-permute-start(f32[3,16,128]{2,1,0:T(8,128)S(1)} %get-tuple-element.44), channel_id=1, source_target_pairs={{0,32},{16,48},{32,64},{48,80},{64,96},{80,112},{96,0},{112,16},{1... | collective-permute-start | bytes 73736 | tf_op jit(solution)/shard_map/ppermute | solution.py:443
  61.0 4.1 %collective-permute-start.11 = (f32[3,16,128]{2,1,0:T(8,128)S(1)}, f32[3,16,128]{2,1,0:T(8,128)S(1)}, u32[]{:S(2)}, u32[]{:S(2)}) collective-permute-start(f32[3,16,128]{2,1,0:T(8,128)S(1)} %get-tuple-element.44), channel_id=1, source_target_pairs={{0,16},{16,0},{32,48},{48,32},{64,80},{80,64},{96,112},{112,96},{1... | collective-permute-start | bytes 73736 | tf_op jit(solution)/shard_map/ppermute | solution.py:438
  61.9 3.2 %collective-permute-start.17 = (f32[3,16,128]{2,1,0:T(8,128)S(1)}, f32[3,16,128]{2,1,0:T(8,128)S(1)}, u32[]{:S(2)}, u32[]{:S(2)}) collective-permute-start(f32[3,16,128]{2,1,0:T(8,128)S(1)} %collective-permute-done.16.refs_9_), channel_id=1, source_target_pairs={{0,16},{16,0},{32,48},{48,32},{64,80},{80,64},{96,112},{112,96},{1... | collective-permute-start | bytes 73736 | tf_op jit(solution)/shard_map/ppermute | solution.py:438
  64.6 1.2 %collective-permute-start.15 = (f32[3,16,128]{2,1,0:T(8,128)S(1)}, f32[3,16,128]{2,1,0:T(8,128)S(1)}, u32[]{:S(2)}, u32[]{:S(2)}) collective-permute-start(f32[3,16,128]{2,1,0:T(8,128)S(1)} %collective-permute-done.14.refs_7_), channel_id=1, source_target_pairs={{0,16},{16,0},{32,48},{48,32},{64,80},{80,64},{96,112},{112,96},{1... | collective-permute-start | bytes 73736 | tf_op jit(solution)/shard_map/ppermute | solution.py:438
  64.9 1.2 %collective-permute-start.13 = (f32[3,16,128]{2,1,0:T(8,128)S(1)}, f32[3,16,128]{2,1,0:T(8,128)S(1)}, u32[]{:S(2)}, u32[]{:S(2)}) collective-permute-start(f32[3,16,128]{2,1,0:T(8,128)S(1)} %collective-permute-done.12.refs_5_), channel_id=1, source_target_pairs={{0,16},{16,0},{32,48},{48,32},{64,80},{80,64},{96,112},{112,96},{1... | collective-permute-start | bytes 73736 | tf_op jit(solution)/shard_map/ppermute | solution.py:438
  72.7 18.0 %all-to-all-start.3 = ((f32[16,3,16,128]{3,2,1,0:T(8,128)}), f32[16,3,16,128]{3,2,1,0:T(8,128)S(1)}, u32[]{:S(2)}, u32[]{:S(2)}) async-start(f32[16,3,16,128]{3,2,1,0:T(8,128)} %bitcast.4), calls=%async_computation.3 | async-start | bytes 786432 | tf_op jit(solution)/shard_map/all_to_all | solution.py:447
  78.6 1.9 %collective-permute-start.18 = (f32[4,3,16,128]{3,2,1,0:T(8,128)S(1)}, f32[4,3,16,128]{3,2,1,0:T(8,128)S(1)}, u32[]{:S(2)}, u32[]{:S(2)}) collective-permute-start(f32[4,3,16,128]{3,2,1,0:T(8,128)S(1)} %get-tuple-element.47), channel_id=1, source_target_pairs={{0,16},{16,0},{32,48},{48,32},{64,80},{80,64},{96,112},{112,96},{1... | collective-permute-start | bytes 294920 | tf_op jit(solution)/shard_map/ppermute | solution.py:438
  80.6 6.7 %collective-permute-start.19 = (f32[3,16,128]{2,1,0:T(8,128)S(1)}, f32[3,16,128]{2,1,0:T(8,128)S(1)}, u32[]{:S(2)}, u32[]{:S(2)}) collective-permute-start(f32[3,16,128]{2,1,0:T(8,128)S(1)} %get-tuple-element.49), channel_id=1, source_target_pairs={{0,32},{16,48},{32,64},{48,80},{64,96},{80,112},{96,0},{112,16},{1... | collective-permute-start | bytes 73736 | tf_op jit(solution)/shard_map/ppermute | solution.py:443
  81.7 7.2 %collective-permute-start.20 = (f32[3,16,128]{2,1,0:T(8,128)S(1)}, f32[3,16,128]{2,1,0:T(8,128)S(1)}, u32[]{:S(2)}, u32[]{:S(2)}) collective-permute-start(f32[3,16,128]{2,1,0:T(8,128)S(1)} %get-tuple-element.50), channel_id=1, source_target_pairs={{0,64},{16,80},{32,96},{48,112},{64,0},{80,16},{96,32},{112,48},{1... | collective-permute-start | bytes 73736 | tf_op jit(solution)/shard_map/ppermute | solution.py:443
  86.9 3.8 %collective-permute-start.21 = (f32[3,16,128]{2,1,0:T(8,128)S(1)}, f32[3,16,128]{2,1,0:T(8,128)S(1)}, u32[]{:S(2)}, u32[]{:S(2)}) collective-permute-start(f32[3,16,128]{2,1,0:T(8,128)S(1)} %get-tuple-element.51), channel_id=1, source_target_pairs={{0,96},{16,112},{32,0},{48,16},{64,32},{80,48},{96,64},{112,80},{1... | collective-permute-start | bytes 73736 | tf_op jit(solution)/shard_map/ppermute | solution.py:443
